TPU v7x, 32 devices: a whole 2x2x4 slice. The times are simulated.
32 devices in a mesh: group: 2 (over y), line: 16 (over z, x, core).
Axes of the slice: x: 2, y: 2, z: 4, core: 2. Of those that a mesh axis runs over, the one named last changes fastest.
Arguments:
- residual_in: bfloat16 [2048, 2048], P(('group', 'line')), parts along dimension 0, may hold values from -6 to 6
- queries: bfloat16 [2048, 2048], P(('group', 'line')), parts along dimension 0, may hold values from -8 to 8
- question_key_values: bfloat16 [2048, 512], P(('group', 'line')), parts along dimension 0, may hold values from -8 to 8
- document_prefix_cache: bfloat16 [4096, 512], P(('group', 'line')), parts along dimension 0, may hold values from -8 to 8
- out_proj: bfloat16 [2048, 2048], P('line'), may hold values from -0.125 to 0.125
- norm_gain: float32 [2048], replicated, may hold values from 0.5 to 1.5
- routes: int32 [2048, 8], P(('group', 'line')), parts along dimension 0, may hold values from 0 to 15, all different within a row; in each aligned block of 32 rows (0 to 31, 32 to 63, ...) at most 32 rows name the same one
- keep_mask: int32 [2048, 8], P(('group', 'line')), parts along dimension 0, may hold values 0 or 1
- route_weights: float32 [2048, 8], P(('group', 'line')), parts along dimension 0, may hold values from 0.02 to 0.4
- expert_slots: int32 [16], replicated, may hold values from 0 to 15, each once
- expert_gate: bfloat16 [16, 2048, 768], P('line'), may hold values from -0.125 to 0.125
- expert_up: bfloat16 [16, 2048, 768], P('line'), may hold values from -0.125 to 0.125
- expert_down: bfloat16 [16, 768, 2048], P('line'), may hold values from -0.21875 to 0.21875
Outputs:
- layer_out: bfloat16 [2048, 2048], P(('group', 'line')), parts along dimension 0
There are 2 independent parts, one for each index of `group`. A program takes and returns all parts, laid end to end along the dimension named above; an argument that names none is the same for every part. Nothing has to cross between parts.
Inputs may be any that keep to these rules, and one draw needn't show every extreme that they name: `routes`: each row names 8 different experts; in every aligned block of half of 64 rows no expert is named by more than 32 rows. `expert_slots`: every slot holds exactly one expert.
All inputs are finite; a program needn't handle non-finite values. No bound on the sum of `keep_mask` on one device may be relied on, other than what follows from the above.
Results may differ from a plain program's by a relative error of at most 0.0045.
Values may be sent and summed in bfloat16 or wider, within the bound.
A program may use at most 256 MiB of HBM per device.

v0:
```python
import math

import jax
import jax.numpy as jnp
from jax import lax
from jax.sharding import PartitionSpec as P

QUERY_HEADS = 16
KEY_VALUE_HEADS = 2
HEAD_SIZE = 128
TOPK = 8
QLEN = 16


def partner(array, axis, bit):
    return lax.ppermute(array, axis, [(i, i ^ 1 << bit) for i in range(lax.axis_size(axis))])


def shifted(value, axis, steps):
    count = lax.axis_size(axis)
    pairs = [(source, (source + steps) % count) for source in range(count)]
    return lax.ppermute(value, axis, pairs)


def expert_answers(received, expert_gate, expert_up, expert_down):
    buffer_shape = received.shape
    flat_rows = received.reshape(-1, buffer_shape[-1])
    gate_proj = jnp.dot(flat_rows, expert_gate[0], preferred_element_type=jnp.float32)
    upper = jnp.dot(flat_rows, expert_up[0], preferred_element_type=jnp.float32)
    middle = (jax.nn.silu(gate_proj) * upper).astype(jnp.bfloat16)
    return (
        jnp.dot(middle, expert_down[0], preferred_element_type=jnp.float32)
        .astype(jnp.bfloat16)
        .reshape(buffer_shape)
    )


def mix_experts(
    normed_rows,
    route_rows,
    keep_rows,
    weight_rows,
    expert_slots,
    expert_gate,
    expert_up,
    expert_down,
    slot_cap,
):
    row_count = normed_rows.shape[0]
    model_width = normed_rows.shape[1]
    line_count = lax.axis_size("line")
    pair_count = row_count * TOPK
    expert_ids = route_rows.reshape(pair_count)
    kept_pairs = keep_rows.reshape(pair_count) > 0
    numbers = jnp.arange(expert_slots.shape[0], dtype=jnp.int32)
    matches = expert_ids[:, None] == numbers[None, :]
    target = jnp.sum(jnp.where(matches, expert_slots[None, :], 0), axis=1)
    chosen = (matches & kept_pairs[:, None]).astype(jnp.bfloat16)
    pair_order = jnp.arange(pair_count, dtype=jnp.int32)
    earlier = (pair_order[:, None] > pair_order[None, :]).astype(jnp.bfloat16)
    before = jnp.dot(earlier, chosen, preferred_element_type=jnp.float32)
    slot_rank = jnp.sum(before * chosen.astype(jnp.float32), axis=1).astype(jnp.int32)
    slot_index = jnp.where(kept_pairs, target * slot_cap + slot_rank, line_count * slot_cap)
    slot_owner = (
        jnp.full((line_count * slot_cap,), pair_count, jnp.int32)
        .at[slot_index]
        .set(pair_order, mode="drop")
    )
    source_row = jnp.where(slot_owner < pair_count, slot_owner // TOPK, row_count)
    padded = jnp.concatenate([normed_rows, jnp.zeros((1, model_width), jnp.bfloat16)], axis=0)
    buffer = padded[source_row].reshape(line_count, slot_cap, model_width)
    returned = lax.all_to_all(
        expert_answers(
            lax.all_to_all(buffer, "line", split_axis=0, concat_axis=0, tiled=True),
            expert_gate,
            expert_up,
            expert_down,
        ),
        "line",
        split_axis=0,
        concat_axis=0,
        tiled=True,
    )
    padded_back = jnp.concatenate(
        [
            returned.reshape(line_count * slot_cap, model_width),
            jnp.zeros((1, model_width), jnp.bfloat16),
        ],
        axis=0,
    )
    per_pair = padded_back[slot_index].reshape(row_count, TOPK, model_width)
    weight = jnp.where(kept_pairs, weight_rows.reshape(pair_count), 0.0).reshape(row_count, TOPK)
    return jnp.sum(per_pair.astype(jnp.float32) * weight[:, :, None], axis=1)


def near_state(heads_of_queries, local_keys, local_values, score_scale):
    local_tokens = heads_of_queries.shape[0]
    near_scores = (
        jnp.einsum(
            "thgd,shd->thgs", heads_of_queries, local_keys, preferred_element_type=jnp.float32
        )
        * score_scale
    )
    position = jnp.arange(local_tokens, dtype=jnp.int32)
    visible_mask = (position[:, None] // QLEN == position[None, :] // QLEN) & (
        position[None, :] <= position[:, None]
    )
    near_scores = jnp.where(visible_mask[:, None, None, :], near_scores, -1e30)
    run_max = near_scores.max(-1)
    exp_terms = jnp.exp(near_scores - run_max[..., None])
    run_sum = exp_terms.sum(-1)
    run_acc = jnp.einsum(
        "thgs,shd->thgd",
        exp_terms.astype(jnp.bfloat16),
        local_values,
        preferred_element_type=jnp.float32,
    )
    return (run_max, run_sum, run_acc)


def fold_block(carry, piece, heads_of_queries, kv_heads, score_scale):
    old_max, old_sum, old_acc = carry
    piece_rows = piece.shape[0]
    piece_keys = piece[:, : kv_heads * HEAD_SIZE].reshape(piece_rows, kv_heads, HEAD_SIZE)
    piece_vals = piece[:, kv_heads * HEAD_SIZE :].reshape(piece_rows, kv_heads, HEAD_SIZE)
    far_scores = (
        jnp.einsum(
            "thgd,nhd->thgn", heads_of_queries, piece_keys, preferred_element_type=jnp.float32
        )
        * score_scale
    )
    new_max = jnp.maximum(old_max, far_scores.max(-1))
    factor = jnp.exp(old_max - new_max)
    far_terms = jnp.exp(far_scores - new_max[..., None])
    new_acc = old_acc * factor[..., None] + jnp.einsum(
        "thgn,nhd->thgd",
        far_terms.astype(jnp.bfloat16),
        piece_vals,
        preferred_element_type=jnp.float32,
    )
    return (new_max, old_sum * factor + far_terms.sum(-1), new_acc)


def body(
    residual_in,
    queries,
    question_key_values,
    document_prefix_cache,
    out_proj,
    norm_gain,
    routes,
    keep_mask,
    route_weights,
    expert_slots,
    expert_gate,
    expert_up,
    expert_down,
):
    local_tokens = queries.shape[0]
    queries_per_key_head = QUERY_HEADS // KEY_VALUE_HEADS
    score_scale = 1.0 / math.sqrt(HEAD_SIZE)
    half_kv = KEY_VALUE_HEADS // 2
    query_width = half_kv * queries_per_key_head * HEAD_SIZE
    kv_width = half_kv * HEAD_SIZE
    member = lax.axis_index("line") % 2
    other = 1 - member
    query_split = queries.reshape(local_tokens, 2, query_width)
    key_split = question_key_values[:, : KEY_VALUE_HEADS * HEAD_SIZE].reshape(
        local_tokens, 2, kv_width
    )
    value_split = question_key_values[:, KEY_VALUE_HEADS * HEAD_SIZE :].reshape(
        local_tokens, 2, kv_width
    )
    own_pack = jnp.concatenate(
        [
            lax.dynamic_index_in_dim(query_split, member, 1, keepdims=False),
            lax.dynamic_index_in_dim(key_split, member, 1, keepdims=False),
            lax.dynamic_index_in_dim(value_split, member, 1, keepdims=False),
        ],
        axis=1,
    )
    send_pack = jnp.concatenate(
        [
            lax.dynamic_index_in_dim(query_split, other, 1, keepdims=False),
            lax.dynamic_index_in_dim(key_split, other, 1, keepdims=False),
            lax.dynamic_index_in_dim(value_split, other, 1, keepdims=False),
        ],
        axis=1,
    )
    partner_pack = partner(send_pack, "line", 0)
    both_pack = jnp.concatenate([own_pack, partner_pack], axis=0)
    pair_rows = both_pack.shape[0]
    heads_of_queries = both_pack[:, :query_width].reshape(
        pair_rows, half_kv, queries_per_key_head, HEAD_SIZE
    )
    local_keys = both_pack[:, query_width : query_width + kv_width].reshape(
        pair_rows, half_kv, HEAD_SIZE
    )
    local_values = both_pack[:, query_width + kv_width :].reshape(pair_rows, half_kv, HEAD_SIZE)
    start_state = near_state(heads_of_queries, local_keys, local_values, score_scale)
    prefix_rows = document_prefix_cache.shape[0]
    document_keys = document_prefix_cache[:, : KEY_VALUE_HEADS * HEAD_SIZE].reshape(
        prefix_rows, 2, kv_width
    )
    document_values = document_prefix_cache[:, KEY_VALUE_HEADS * HEAD_SIZE :].reshape(
        prefix_rows, 2, kv_width
    )
    own_slab = jnp.concatenate(
        [
            lax.dynamic_index_in_dim(document_keys, member, 1, keepdims=False),
            lax.dynamic_index_in_dim(document_values, member, 1, keepdims=False),
        ],
        axis=1,
    )
    send_slab = jnp.concatenate(
        [
            lax.dynamic_index_in_dim(document_keys, other, 1, keepdims=False),
            lax.dynamic_index_in_dim(document_values, other, 1, keepdims=False),
        ],
        axis=1,
    )
    slab = jnp.concatenate([own_slab, partner(send_slab, "line", 0)], axis=0)
    levels = (lax.axis_size("line") // 2).bit_length() - 1
    for level in range(levels):
        slab = jnp.concatenate([slab, shifted(slab, "line", 2 * (1 << level))], axis=0)
    slab_rows = slab.shape[0]
    block_rows = math.gcd(slab_rows, 2048)
    slab_blocks = slab.reshape(slab_rows // block_rows, block_rows, 2 * kv_width)

    def scan_step(carry, piece):
        return (fold_block(carry, piece, heads_of_queries, half_kv, score_scale), None)

    final_state, unused = lax.scan(scan_step, start_state, slab_blocks)
    run_max, run_sum, run_acc = final_state
    pair_context = (
        (run_acc / run_sum[..., None]).reshape(pair_rows, query_width).astype(jnp.bfloat16)
    )
    mine = pair_context[:local_tokens]
    returned_context = partner(pair_context[local_tokens:], "line", 0)
    context_rows = jnp.where(
        member == 0,
        jnp.concatenate([mine, returned_context], axis=1),
        jnp.concatenate([returned_context, mine], axis=1),
    )
    attended = jnp.dot(
        context_rows,
        lax.all_gather(out_proj, "line", axis=0, tiled=True),
        preferred_element_type=jnp.float32,
    )
    mixture = residual_in.astype(jnp.float32) + attended
    normed = (
        mixture * lax.rsqrt(jnp.mean(mixture * mixture, axis=-1, keepdims=True) + 1e-06) * norm_gain
    ).astype(jnp.bfloat16)
    half_cap = local_tokens * TOPK // expert_slots.shape[0]
    expert_sum = mix_experts(
        normed,
        routes,
        keep_mask,
        route_weights,
        expert_slots,
        expert_gate,
        expert_up,
        expert_down,
        2 * half_cap,
    )
    return (mixture + expert_sum).astype(jnp.bfloat16)


def solution(mesh):
    placed = (
        P(("group", "line"), None),
        P(("group", "line"), None),
        P(("group", "line"), None),
        P(("group", "line"), None),
        P("line", None),
        P(),
        P(("group", "line"), None),
        P(("group", "line"), None),
        P(("group", "line"), None),
        P(),
        P("line", None, None),
        P("line", None, None),
        P("line", None, None),
    )
    return jax.shard_map(
        body, mesh=mesh, in_specs=placed, out_specs=P(("group", "line"), None), check_vma=False
    )
```

profile of v0, /device:TPU:10, one launch (start us, length us, event | category | flops | bytes accessed | tf_op | source)
XLA Modules:
  0.0 362.9 jit_solution(6563794118542644091)
XLA Ops:
  6.6 0.7 all-gather.2.cloned.1.call-update
  7.3 1.0 fusion.69
  8.4 0.9 constant_dynamic-slice_fusion
  9.3 0.6 pad_maximum_fusion.7
  9.9 1.1 reshape.322
  11.1 1.3 constant_dynamic-slice_fusion.9
  12.4 0.8 fusion.70
  13.4 0.7 pad_maximum_fusion.5
  15.3 0.7 gt.43
  16.2 1.0 fusion.24
  17.3 0.7 fusion.39
  18.1 0.9 copy.82
  19.0 1.6 collective-permute-start.2
  21.2 8.0 %collective-permute-done.2 = bf16[256,256]{1,0:T(8,128)(2,1)S(1)} collective-permute-done((bf16[256,256]{1,0:T(8,128)(2,1)S(1)}, bf16[256,256]{1,0:T(8,128)(2,1)S(1)}, u32[]{:S(2)}, u32[]{:S(2)}) %collective-permute-start.2) | collective-permute-done | bytes 131104 | tf_op jit(solution)/shard_map/ppermute | solution.py:22
  29.2 0.6 copy-done.4
  29.8 0.7 pad_maximum_fusion.4
  30.6 1.3 collective-permute-start.3
  32.5 1.0 copy.79
  33.6 3.0 scatter_custom_fusion
  36.6 1.5 constant_dynamic-update-slice_fusion.3
  38.0 0.7 copy-done.8
  38.7 0.7 pad_maximum_fusion.1
  39.4 1.1 copy.33
  40.6 4.7 %collective-permute-done.3 = bf16[512,256]{1,0:T(8,128)(2,1)} collective-permute-done((bf16[512,256]{1,0:T(8,128)(2,1)}, bf16[512,256]{1,0:T(8,128)(2,1)}, u32[]{:S(2)}, u32[]{:S(2)}) %collective-permute-start.3) | collective-permute-done | bytes 262176 | tf_op jit(solution)/shard_map/ppermute | solution.py:22
  45.3 1.0 pad_maximum_fusion
  46.3 3.4 collective-permute-start.4
  49.8 1.0 fusion.71
  50.8 1.6 constant_dynamic-update-slice_fusion.2
  52.4 1.8 constant_dynamic-update-slice_fusion.1
  54.2 46.1 %collective-permute-done.4 = bf16[1024,256]{1,0:T(8,128)(2,1)S(1)} collective-permute-done((bf16[1024,256]{1,0:T(8,128)(2,1)S(1)}, bf16[1024,256]{1,0:T(8,128)(2,1)S(1)}, u32[]{:S(2)}, u32[]{:S(2)}) %collective-permute-start.4) | collective-permute-done | bytes 524320 | tf_op jit(solution)/shard_map/ppermute | solution.py:22
  100.3 0.8 constant_dynamic-update-slice_fusion
  101.1 2.3 bitcast_reduce_fusion
  103.4 1.4 fusion.1
  104.9 2.2 fusion.14
  107.9 1.2 collective-permute-done.5
  109.1 5.1 %multiply_reduce_fusion = (f32[64]{0:T(128)S(1)}, f32[64,2048]{1,0:T(8,128)S(1)}) fusion(bf16[2048,2048]{1,0:T(8,128)(2,1)} %all-gather.2.cloned.1.call-done, bf16[64,1024]{1,0:T(8,128)(2,1)S(1)} %collective-permute-done.5, bf16[64,1024]{1,0:T(8,128)(2,1)S(1)} %bitcast.150, pred[]{:T(512)S(6)} %eq.37, bf16[64,2048]{1,0:T(8,128)(2,1)} %param.13), kind=kOutput, calls=%fused_computation.39 | convolution fusion | flops 538574784 | bytes 9437441 | tf_op jit(solution)/shard_map/dot_general | solution.py:245
  114.2 0.8 copy-done.1
  115.2 6.0 %gather_fusion = bf16[1024,2048]{1,0:T(8,128)(2,1)} fusion(bf16[65,2048]{1,0:T(8,128)(2,1)S(1)} %concatenate.53, s32[1024]{0:T(1024)S(1)} %fusion.59), kind=kCustom, calls=%fused_computation | custom fusion | bytes 8392704 | tf_op jit(solution)/shard_map/gather | solution.py:71
  121.2 99.6 %all_to_all.10 = bf16[16,64,2048]{2,1,0:T(8,128)(2,1)S(1)} all-to-all(bf16[16,64,2048]{2,1,0:T(8,128)(2,1)} %bitcast.133), channel_id=1, replica_groups=mesh['group'=2,'line'=16] {'line'}, dimensions={0} | all-to-all | bytes 8388608 | tf_op jit(solution)/shard_map/all_to_all | solution.py:74
  220.8 2.0 copy-done.2
  222.7 5.1 %fusion.8 = f32[1024,768]{1,0:T(8,128)} fusion(bf16[1024,2048]{1,0:T(8,128)(2,1)S(1)} %bitcast.135, bf16[1,2048,768]{2,1,0:T(8,128)(2,1)S(1)} %copy-done.20), kind=kOutput, calls=%fused_computation.14 | convolution fusion | flops 3221225472 | bytes 10485760 | tf_op jit(solution)/shard_map/dot_general | solution.py:29
  227.9 12.3 %convolution_convert_fusion = bf16[1024,2048]{1,0:T(8,128)(2,1)} fusion(bf16[1,768,2048]{2,1,0:T(8,128)(2,1)S(1)} %copy-done, f32[1024,768]{1,0:T(8,128)} %fusion.8, bf16[1024,2048]{1,0:T(8,128)(2,1)} %bitcast.136, bf16[1,2048,768]{2,1,0:T(8,128)(2,1)} %param.23), kind=kOutput, calls=%fused_computation.12 | convolution fusion | flops 6449266688 | bytes 17825792 | tf_op jit(solution)/shard_map/dot_general | solution.py:32
  240.2 5.6 %all-to-all-start.1 = ((bf16[16,64,2048]{2,1,0:T(8,128)(2,1)}), bf16[16,64,2048]{2,1,0:T(8,128)(2,1)}, u32[]{:S(2)}, u32[]{:S(2)}) async-start(bf16[16,64,2048]{2,1,0:T(8,128)(2,1)} %bitcast.134), calls=%async_computation.1 | async-start | bytes 8388608 | tf_op jit(solution)/shard_map/all_to_all | solution.py:72
  245.9 92.2 %all-to-all-done.1 = bf16[16,64,2048]{2,1,0:T(8,128)(2,1)} async-done(((bf16[16,64,2048]{2,1,0:T(8,128)(2,1)}), bf16[16,64,2048]{2,1,0:T(8,128)(2,1)}, u32[]{:S(2)}, u32[]{:S(2)}) %all-to-all-start.1) | async-done | bytes 4194336 | tf_op jit(solution)/shard_map/all_to_all | solution.py:72
  338.1 4.7 %concatenate.54 = bf16[1025,2048]{1,0:T(8,128)(2,1)} pad(bf16[1024,2048]{1,0:T(8,128)(2,1)} %bitcast.33, bf16[]{:T(256)} %constant.122.clone.1), padding=0_1x0_0 | pad | bytes 8392706 | tf_op jit(solution)/shard_map/concatenate | solution.py:84
  342.8 8.0 %gather_fusion.1 = bf16[512,2048]{1,0:T(8,128)(2,1)} fusion(bf16[1025,2048]{1,0:T(8,128)(2,1)} %concatenate.54, s32[1024]{0:T(1024)S(1)} %pad_clamp_fusion), kind=kCustom, calls=%fused_computation.1 | custom fusion | bytes 4196352 | tf_op jit(solution)/shard_map/gather | solution.py:91
  350.8 3.4 fusion.4
  354.3 1.8 add_convert_fusion
  (85 shorter events, 4.3 us)
Async XLA Ops:
  6.5 221.3 %copy-start = (bf16[1,768,2048]{2,1,0:T(8,128)(2,1)S(1)}, bf16[1,768,2048]{2,1,0:T(8,128)(2,1)}, u32[]{:S(2)}) copy-start(bf16[1,768,2048]{2,1,0:T(8,128)(2,1)} %param.25) | copy-start | bytes 9437188
  6.5 8.0 %copy-start.18 = (s32[64,8]{0,1:T(8,128)S(1)}, s32[64,8]{0,1:T(8,128)}, u32[]{:S(2)}) copy-start(s32[64,8]{0,1:T(8,128)} %param.20) | copy-start | bytes 6148
  6.5 8.0 %copy-start.17 = (f32[64,8]{0,1:T(8,128)S(1)}, f32[64,8]{0,1:T(8,128)}, u32[]{:S(2)}) copy-start(f32[64,8]{0,1:T(8,128)} %param.21) | copy-start | bytes 6148
  6.5 9.4 %copy-start.16 = (s32[64,8]{0,1:T(8,128)S(1)}, s32[64,8]{0,1:T(8,128)}, u32[]{:S(2)}) copy-start(s32[64,8]{0,1:T(8,128)} %param.19) | copy-start | bytes 6148
  6.5 9.6 %copy-start.19 = (s32[16]{0:T(128)S(1)}, s32[16]{0:T(128)}, u32[]{:S(2)}) copy-start(s32[16]{0:T(128)} %param.22) | copy-start | bytes 196
  6.5 102.6 %all-gather.2.cloned.1.call-start = ((), (), s32[]{:S(2)}) async-start(), calls=%async_computation.2 | async-start | bytes 8912896 | tf_op jit(solution)/shard_map/all_gather | solution.py:247
  9.9 9.0 %collective-permute-start.1 = (bf16[128,256]{1,0:T(8,128)(2,1)}, bf16[128,256]{1,0:T(8,128)(2,1)S(1)}, u32[]{:S(2)}, u32[]{:S(2)}) collective-permute-start(bf16[128,256]{1,0:T(8,128)(2,1)} %pad_maximum_fusion.7), channel_id=1, source_target_pairs={{0,1},{1,0},{2,3},{3,2},{4,5},{5,4},{6,7},{7,6},{8,9},{9,8},{10,11... | collective-permute-start | bytes 196616 | tf_op jit(solution)/shard_map/ppermute | solution.py:16
  14.0 24.0 %collective-permute-start = (bf16[64,1280]{1,0:T(8,128)(2,1)}, bf16[64,1280]{1,0:T(8,128)(2,1)S(1)}, u32[]{:S(2)}, u32[]{:S(2)}) collective-permute-start(bf16[64,1280]{1,0:T(8,128)(2,1)} %pad_maximum_fusion.5), channel_id=1, source_target_pairs={{0,1},{1,0},{2,3},{3,2},{4,5},{5,4},{6,7},{7,6},{8,9},{9,8},{10,11... | collective-permute-start | bytes 491528 | tf_op jit(solution)/shard_map/ppermute | solution.py:16
  18.9 13.0 %copy-start.6 = (bf16[128,1,128]{2,0,1:T(8,128)(2,1)}, bf16[128,1,128]{2,0,1:T(8,128)(2,1)S(1)}, u32[]{:S(2)}) copy-start(bf16[128,1,128]{2,0,1:T(8,128)(2,1)S(1)} %copy.82) | copy-start | bytes 98308
  18.9 13.0 %copy-start.7 = (bf16[128,1,128]{2,0,1:T(8,128)(2,1)}, bf16[128,1,128]{2,0,1:T(8,128)(2,1)S(1)}, u32[]{:S(2)}) copy-start(bf16[128,1,128]{2,0,1:T(8,128)(2,1)S(1)} %copy.83) | copy-start | bytes 98308
  19.0 13.6 %copy-start.5 = (bf16[128,256]{1,0:T(8,128)(2,1)}, bf16[128,256]{1,0:T(8,128)(2,1)S(1)}, u32[]{:S(2)}) copy-start(bf16[128,256]{1,0:T(8,128)(2,1)S(1)} %collective-permute-done.1) | copy-start | bytes 196612
  19.0 10.2 %collective-permute-start.2 = (bf16[256,256]{1,0:T(8,128)(2,1)S(1)}, bf16[256,256]{1,0:T(8,128)(2,1)S(1)}, u32[]{:S(2)}, u32[]{:S(2)}) collective-permute-start(bf16[256,256]{1,0:T(8,128)(2,1)S(1)} %pad_maximum_fusion.6), channel_id=1, source_target_pairs={{0,2},{1,3},{2,4},{3,5},{4,6},{5,7},{6,8},{7,9},{8,10},{9,11},{10,... | collective-permute-start | bytes 393224 | tf_op jit(solution)/shard_map/ppermute | solution.py:22
  29.2 0.7 copy-start.4
  30.6 14.7 %collective-permute-start.3 = (bf16[512,256]{1,0:T(8,128)(2,1)}, bf16[512,256]{1,0:T(8,128)(2,1)}, u32[]{:S(2)}, u32[]{:S(2)}) collective-permute-start(bf16[512,256]{1,0:T(8,128)(2,1)} %pad_maximum_fusion.4), channel_id=1, source_target_pairs={{0,4},{1,5},{2,6},{3,7},{4,8},{5,9},{6,10},{7,11},{8,12},{9,13},{1... | collective-permute-start | bytes 786440 | tf_op jit(solution)/shard_map/ppermute | solution.py:22
  33.5 4.5 %copy-start.10 = (bf16[64,1,128]{2,0,1:T(8,128)(2,1)}, bf16[64,1,128]{2,0,1:T(8,128)(2,1)S(1)}, u32[]{:S(2)}) copy-start(bf16[64,1,128]{2,0,1:T(8,128)(2,1)S(1)} %copy.87) | copy-start | bytes 49156
  38.0 0.7 copy-start.8
  46.3 53.9 %collective-permute-start.4 = (bf16[1024,256]{1,0:T(8,128)(2,1)S(1)}, bf16[1024,256]{1,0:T(8,128)(2,1)S(1)}, u32[]{:S(2)}, u32[]{:S(2)}) collective-permute-start(bf16[1024,256]{1,0:T(8,128)(2,1)S(1)} %pad_maximum_fusion), channel_id=1, source_target_pairs={{0,8},{1,9},{2,10},{3,11},{4,12},{5,13},{6,14},{7,15},{8,0},{9,1},... | collective-permute-start | bytes 1572872 | tf_op jit(solution)/shard_map/ppermute | solution.py:22
  103.4 1.4 copy-start.3
  104.8 2.2 copy-start.9
  104.8 2.2 copy-start.11
  104.8 2.9 copy-start.13
  107.7 1.4 collective-permute-start.5
  109.1 5.9 %copy-start.14 = (f32[2048]{0:T(1024)S(1)}, f32[2048]{0:T(1024)}, u32[]{:S(2)}) copy-start(f32[2048]{0:T(1024)} %param.18) | copy-start | bytes 24580
  114.2 0.8 copy-start.1
  121.2 101.6 %copy-start.20 = (bf16[1,2048,768]{2,1,0:T(8,128)(2,1)S(1)}, bf16[1,2048,768]{2,1,0:T(8,128)(2,1)}, u32[]{:S(2)}) copy-start(bf16[1,2048,768]{2,1,0:T(8,128)(2,1)} %param.24) | copy-start | bytes 9437188
  220.8 2.0 copy-start.2
  240.2 5.6 %copy-start.12 = (f32[64,8]{0,1:T(8,128)S(1)}, f32[64,8]{0,1:T(8,128)}, u32[]{:S(2)}) copy-start(f32[64,8]{0,1:T(8,128)} %get-tuple-element.15) | copy-start | bytes 6148
  240.2 5.7 %copy-start.15 = (s32[512,1]{0,1:T(1,128)S(1)}, s32[512,1]{0,1:T(1,128)}, u32[]{:S(2)}) copy-start(s32[512,1]{0,1:T(1,128)} %get-tuple-element.43) | copy-start | bytes 6148
  240.2 97.9 %all-to-all-start.1 = ((bf16[16,64,2048]{2,1,0:T(8,128)(2,1)}), bf16[16,64,2048]{2,1,0:T(8,128)(2,1)}, u32[]{:S(2)}, u32[]{:S(2)}) async-start(bf16[16,64,2048]{2,1,0:T(8,128)(2,1)} %bitcast.134), calls=%async_computation.1 | async-start | bytes 8388608 | tf_op jit(solution)/shard_map/all_to_all | solution.py:72
Sparse Core Ops, SparseCore 0:
  9.5 96.4 all-gather.1
where the time goes:
time: 364 us; the launch traced here: 363 us
  waiting for transfers between devices  153 us (42%)
  blocking collectives  99.6 us (27%)
  local copies, waits for them, and re-layouts  41.3 us (11%)
  matrix products  29.5 us (8%)
  between operations  13.8 us (4%)
  other arithmetic  13.3 us (4%)
  starting transfers between devices  12.5 us (3%)
    all_to_all x1, blocking collectives, mix_experts(): lax.all_to_all(buffer, 'line', split_axis=0, concat_axis=0, tiled=True)  99.6 us
    all_to_all x1, waiting for transfers between devices, mix_experts(): lax.all_to_all(expert_answers(lax.all_to_all(buffer, 'line', split_axis=0...  92.2 us
    ppermute x3, waiting for transfers between devices, shifted(): return lax.ppermute(value, axis, pairs)  58.9 us
    dot_general x1, matrix products, expert_answers(): jnp.dot(middle, expert_down[0], preferred_element_type=jnp.float32)  12.3 us
    unnamed x58, local copies, waits for them, and re-layouts  11 us
    gather x1, local copies, waits for them, and re-layouts, mix_experts(): per_pair = padded_back[slot_index].reshape(row_count, TOPK, model_width)  8 us
  transfers between devices with their start and end apart: 8, of which 5 were waited for; matrix products, arithmetic and copies ran while one was open for 9% of the time, Pallas kernels for 0%

commit v1 on v0

v1 whole, which is shorter than its diff:
```python
import math

import jax
import jax.numpy as jnp
from jax import lax
from jax.sharding import PartitionSpec as P

QUERY_HEADS = 16
KEY_VALUE_HEADS = 2
HEAD_SIZE = 128
QLEN = 16


def attention(queries, local_kv, prefix):
    tokens = queries.shape[0]
    group = QUERY_HEADS // KEY_VALUE_HEADS
    scale = 1.0 / math.sqrt(HEAD_SIZE)
    width = KEY_VALUE_HEADS * HEAD_SIZE
    heads = queries.reshape(tokens, KEY_VALUE_HEADS, group, HEAD_SIZE)
    near_k = local_kv[:, :width].reshape(tokens, KEY_VALUE_HEADS, HEAD_SIZE)
    near_v = local_kv[:, width:].reshape(tokens, KEY_VALUE_HEADS, HEAD_SIZE)
    near = (
        jnp.einsum("thgd,shd->thgs", heads, near_k, preferred_element_type=jnp.float32) * scale
    )
    position = jnp.arange(tokens, dtype=jnp.int32)
    visible = (position[:, None] // QLEN == position[None, :] // QLEN) & (
        position[None, :] <= position[:, None]
    )
    near = jnp.where(visible[:, None, None, :], near, -1e30)
    top = near.max(-1)
    terms = jnp.exp(near - top[..., None])
    total = terms.sum(-1)
    acc = jnp.einsum(
        "thgs,shd->thgd", terms.astype(jnp.bfloat16), near_v, preferred_element_type=jnp.float32
    )
    rows = prefix.shape[0]
    block = math.gcd(rows, 2048)

    def step(carry, piece):
        old_max, old_sum, old_acc = carry
        keys = piece[:, :width].reshape(block, KEY_VALUE_HEADS, HEAD_SIZE)
        values = piece[:, width:].reshape(block, KEY_VALUE_HEADS, HEAD_SIZE)
        far = jnp.einsum("thgd,nhd->thgn", heads, keys, preferred_element_type=jnp.float32) * scale
        new_max = jnp.maximum(old_max, far.max(-1))
        factor = jnp.exp(old_max - new_max)
        far = jnp.exp(far - new_max[..., None])
        new_acc = old_acc * factor[..., None] + jnp.einsum(
            "thgn,nhd->thgd", far.astype(jnp.bfloat16), values, preferred_element_type=jnp.float32
        )
        return (new_max, old_sum * factor + far.sum(-1), new_acc), None

    (top, total, acc), _ = lax.scan(
        step, (top, total, acc), prefix.reshape(rows // block, block, 2 * width)
    )
    return (acc / total[..., None]).reshape(tokens, QUERY_HEADS * HEAD_SIZE).astype(jnp.bfloat16)


def body(
    residual_in,
    queries,
    question_key_values,
    document_prefix_cache,
    out_proj,
    norm_gain,
    routes,
    keep_mask,
    route_weights,
    expert_slots,
    expert_gate,
    expert_up,
    expert_down,
):
    prefix = lax.all_gather(document_prefix_cache, "line", axis=0, tiled=True)
    projection = lax.all_gather(out_proj, "line", axis=0, tiled=True)
    numbers = jnp.arange(expert_slots.shape[0], dtype=jnp.int32)
    slot_of_number = expert_slots[None, :] == numbers[:, None]
    number_of_slot = jnp.sum(jnp.where(slot_of_number, numbers[None, :], 0), axis=1)
    kept = jnp.where(keep_mask > 0, route_weights, 0.0)
    per_slot = jnp.sum(
        jnp.where(routes[:, :, None] == number_of_slot[None, None, :], kept[:, :, None], 0.0),
        axis=1,
    )
    all_slots = lax.all_gather(per_slot, "line", axis=0, tiled=True)
    weight = lax.dynamic_slice_in_dim(all_slots, lax.axis_index("line"), 1, 1)
    context = attention(queries, question_key_values, prefix)
    attended = jnp.dot(context, projection, preferred_element_type=jnp.float32)
    mixture = residual_in.astype(jnp.float32) + attended
    normed = (
        mixture * lax.rsqrt(jnp.mean(mixture * mixture, axis=-1, keepdims=True) + 1e-06) * norm_gain
    ).astype(jnp.bfloat16)
    rows = lax.all_gather(normed, "line", axis=0, tiled=True)
    gate = jnp.dot(rows, expert_gate[0], preferred_element_type=jnp.float32)
    upper = jnp.dot(rows, expert_up[0], preferred_element_type=jnp.float32)
    middle = (jax.nn.silu(gate) * upper).astype(jnp.bfloat16)
    answer = jnp.dot(middle, expert_down[0], preferred_element_type=jnp.float32)
    share = (answer.astype(jnp.bfloat16).astype(jnp.float32) * weight).astype(jnp.bfloat16)
    summed = lax.psum_scatter(share, "line", scatter_dimension=0, tiled=True)
    return (mixture + summed.astype(jnp.float32)).astype(jnp.bfloat16)


def solution(mesh):
    rows = P(("group", "line"), None)
    expert = P("line", None, None)
    placed = (rows, rows, rows, rows, P("line", None), P(), rows, rows, rows, P())
    return jax.shard_map(
        body,
        mesh=mesh,
        in_specs=placed + (expert, expert, expert),
        out_specs=rows,
        check_vma=False,
    )
```

time: 364 us -> 286 us (0.79)
  blocking collectives: 99.6 us -> 17 us
  waiting for transfers between devices: 153 us -> 203 us
  local copies, waits for them, and re-layouts: 41.3 us -> 10.8 us
  starting transfers between devices: 12.5 us -> 0.12 us
  other arithmetic: 13.3 us -> 5.47 us
  matrix products: 29.5 us -> 33.6 us
    all_gather x1 -> x3, waiting for transfers between devices: 0.01 us -> 131 us  [the longest x1 61.3 us: body(): projection = lax.all_gather(out_proj, 'line', axis=0, tiled=True)]
    all_to_all x1 -> x0, blocking collectives: 99.6 us -> none  [mix_experts(): lax.all_to_all(buffer, 'line', split_axis=0, concat_axis=0, tiled=True)]
    all_to_all x1 -> x0, waiting for transfers between devices: 92.2 us -> none  [mix_experts(): lax.all_to_all(expert_answers(lax.all_to_all(buffer, 'line', split_axis=0...]
    reduce_scatter x0 -> x1, waiting for transfers between devices: none -> 71.8 us  [body(): summed = lax.psum_scatter(share, 'line', scatter_dimension=0, tiled=True)]
    ppermute x6 -> x0, waiting for transfers between devices: 60.1 us -> none  [the longest x3 58.9 us: shifted(): return lax.ppermute(value, axis, pairs)]
    all_gather x0 -> x1, blocking collectives: none -> 17 us  [body(): all_slots = lax.all_gather(per_slot, 'line', axis=0, tiled=True)]
    gather x2 -> x0, local copies, waits for them, and re-layouts: 14 us -> none  [the longest x1 8 us: mix_experts(): per_pair = padded_back[slot_index].reshape(row_count, TOPK, model_width)]
    ppermute x6 -> x0, starting transfers between devices: 6.9 us -> none  [the longest x3 6.32 us: shifted(): return lax.ppermute(value, axis, pairs)]
  transfers between devices with their start and end apart: 8 -> 4, of which waited for: 5 -> 4; matrix products, arithmetic and copies ran while one was open for 9% -> 6% of each run, Pallas kernels for 0% -> 0%
where the time goes in v1:
time: 286 us; the launch traced here: 284 us
  waiting for transfers between devices  203 us (71%)
  matrix products  33.6 us (12%)
  blocking collectives  17 us (6%)
  between operations  13.3 us (5%)
  local copies, waits for them, and re-layouts  10.8 us (4%)
  other arithmetic  5.47 us (2%)
    reduce_scatter x1, waiting for transfers between devices, body(): summed = lax.psum_scatter(share, 'line', scatter_dimension=0, tiled=True)  71.8 us
    all_gather x1, waiting for transfers between devices, body(): projection = lax.all_gather(out_proj, 'line', axis=0, tiled=True)  61.3 us
    all_gather x1, waiting for transfers between devices, body(): prefix = lax.all_gather(document_prefix_cache, 'line', axis=0, tiled=True)  37.3 us
    all_gather x1, waiting for transfers between devices, body(): rows = lax.all_gather(normed, 'line', axis=0, tiled=True)  32.3 us
    all_gather x1, blocking collectives, body(): all_slots = lax.all_gather(per_slot, 'line', axis=0, tiled=True)  17 us
    dot_general x1, matrix products, body(): answer = jnp.dot(middle, expert_down[0], preferred_element_type=jnp.float32)  12.3 us
    dot_general x1, matrix products, body(): upper = jnp.dot(rows, expert_up[0], preferred_element_type=jnp.float32)  8.31 us
  transfers between devices with their start and end apart: 4, of which 4 were waited for; matrix products, arithmetic and copies ran while one was open for 6% of the time, Pallas kernels for 0%

profile of v1, /device:TPU:10, one launch (start us, length us, event | category | flops | bytes accessed | tf_op | source)
XLA Modules:
  0.0 283.8 jit_solution(6150841262574367657)
XLA Ops:
  6.5 0.0 copy-start
  6.5 0.0 all-gather.5.cloned.1.call-start
  6.5 1.8 copy.69
  8.3 0.0 all-gather.5.cloned.1.call-update
  8.4 0.0 all-gather.7.cloned.1.call-start
  8.4 0.7 all-gather.7.cloned.1.call-update
  9.1 0.0 all-gather.9.cloned.1.call-start
  9.2 1.0 copy.90
  10.2 0.8 fusion.35
  11.0 0.1 fusion.31
  11.1 0.4 fusion.36
  11.5 0.8 fusion.22
  12.3 1.8 copy.67
  14.1 37.3 %all-gather.5.cloned.1.call-done = bf16[2048,512]{0,1:T(8,128)(2,1)} async-done(((bf16[128,512]{0,1:T(8,128)(2,1)}), bf16[2048,512]{0,1:T(8,128)(2,1)}) %all-gather.5.cloned.1.call-update) | async-done | bytes 2097168 | tf_op jit(solution)/shard_map/all_gather | solution.py:73
  51.5 2.7 fusion.34
  54.2 1.3 bitcast_reduce_fusion
  55.5 0.0 copy-start.1
  55.5 1.7 fusion.1
  57.2 1.5 copy-done.1
  58.7 0.1 copy.72
  58.8 0.1 copy.75
  58.9 0.0 copy-start.3
  58.9 5.7 %fusion.3 = f32[2,64,8,128]{3,1,2,0:T(8,128)S(1)} fusion(bf16[2048,2,128,1]{0,2,3,1:T(8,128)(2,1)} %bitcast.72, f32[2,2048,64,8]{1,2,3,0:T(8,128)} %copy-done.1, f32[64,2,8]{0,2,1:T(8,128)S(1)} %max.14), kind=kOutput, calls=%fused_computation.6 | convolution fusion | flops 543162368 | bytes 9965568 | tf_op jit(solution)/shard_map/while/body/eval_jaxpr/thgn,nhd->thgd/dot_general | solution.py:47
  64.6 0.0 copy-done.3
  64.6 0.5 fusion.19
  65.1 61.3 %all-gather.7.cloned.1.call-done = bf16[2048,2048]{1,0:T(8,128)(2,1)} async-done(((bf16[128,2048]{1,0:T(8,128)(2,1)}), bf16[2048,2048]{1,0:T(8,128)(2,1)}) %all-gather.7.cloned.1.call-update) | async-done | bytes 8388624 | tf_op jit(solution)/shard_map/all_gather | solution.py:74
  126.4 5.1 %multiply_reduce_fusion = (f32[64]{0:T(128)S(1)}, f32[64,2048]{1,0:T(8,128)S(1)}) fusion(bf16[2048,2048]{1,0:T(8,128)(2,1)} %all-gather.7.cloned.1.call-done, bf16[8,8,16,128]{3,2,1,0:T(8,128)(2,1)S(1)} %bitcast.75, bf16[64,2048]{1,0:T(8,128)(2,1)} %param.13), kind=kOutput, calls=%fused_computation.26 | convolution fusion | flops 537395136 | bytes 9437440 | tf_op jit(solution)/shard_map/dot_general | solution.py:86
  131.5 0.0 copy-start.2
  131.6 0.8 copy-done.2
  132.3 0.0 copy-done.4
  132.3 0.8 multiply_convert_fusion.2
  133.2 0.0 all-gather.9.cloned.1.call-update
  133.2 0.0 reduce-scatter.2.cloned.1.call-start
  133.2 0.0 copy-done.8
  133.2 0.1 select_reduce_fusion.1
  133.4 0.0 copy-done.5
  133.4 0.0 copy-done.6
  133.4 0.0 copy-done.7
  133.4 0.1 select_reduce_fusion
  133.5 17.0 %all-gather = f32[16,64,16]{1,2,0:T(8,128)S(1)} all-gather(f32[1,64,16]{1,2,0:T(8,128)S(1)} %bitcast.78), channel_id=1, replica_groups=mesh['group'=2,'line'=16] {'line'}, dimensions={0}, use_global_device_ids=true | all-gather | bytes 69632 | tf_op jit(solution)/shard_map/all_gather | solution.py:83
  150.6 0.1 reshape.172
  150.7 32.3 %all-gather.9.cloned.1.call-done = bf16[1024,2048]{1,0:T(8,128)(2,1)} async-done(((bf16[64,2048]{1,0:T(8,128)(2,1)}), bf16[1024,2048]{1,0:T(8,128)(2,1)}) %all-gather.9.cloned.1.call-update) | async-done | bytes 4194320 | tf_op jit(solution)/shard_map/all_gather | solution.py:91
  183.0 8.3 %fusion.8 = f32[1024,768]{1,0:T(8,128)} fusion(bf16[1024,2048]{1,0:T(8,128)(2,1)} %all-gather.9.cloned.1.call-done, bf16[1,2048,768]{2,1,0:T(8,128)(2,1)} %param.24), kind=kOutput, calls=%fused_computation.10 | convolution fusion | flops 3221225472 | bytes 10485760 | tf_op jit(solution)/shard_map/dot_general | solution.py:93
  191.3 0.0 copy-done
  191.3 12.3 %multiply_convert_fusion = bf16[1024,2048]{1,0:T(8,128)(2,1)} fusion(f32[1024]{0:T(1024)S(1)} %bitcast.80, bf16[1,768,2048]{2,1,0:T(8,128)(2,1)S(1)} %copy-done, f32[1024,768]{1,0:T(8,128)} %fusion.8, bf16[1024,2048]{1,0:T(8,128)(2,1)} %all-gather.9.cloned.1.call-done, bf16[1,2048,768]{2,1,0:T(8,128)(2,1)} %param.23), kind=kOutput, calls=%fused_computation.3 | convolution fusion | flops 6455558144 | bytes 17829888 | tf_op jit(solution)/shard_map/dot_general | solution.py:95
  203.6 0.0 reduce-scatter.2.cloned.1.call-update
  203.6 71.8 %reduce-scatter.2.cloned.1.call-done = bf16[64,2048]{1,0:T(8,128)(2,1)} async-done(((bf16[1024,2048]{1,0:T(8,128)(2,1)}), bf16[64,2048]{1,0:T(8,128)(2,1)}) %reduce-scatter.2.cloned.1.call-update) | async-done | bytes 262160 | tf_op jit(solution)/shard_map/reduce_scatter | solution.py:97
  275.4 1.9 add_convert_fusion
  (15 shorter events, 0.2 us)
Async XLA Ops:
  6.5 184.8 %copy-start = (bf16[1,768,2048]{2,1,0:T(8,128)(2,1)S(1)}, bf16[1,768,2048]{2,1,0:T(8,128)(2,1)}, u32[]{:S(2)}) copy-start(bf16[1,768,2048]{2,1,0:T(8,128)(2,1)} %param.25) | copy-start | bytes 9437188
  6.5 44.9 %all-gather.5.cloned.1.call-start = ((), (), s32[]{:S(2)}) async-start(), calls=%async_computation.1 | async-start | bytes 2228224 | tf_op jit(solution)/shard_map/all_gather | solution.py:73
  8.4 118.0 %all-gather.7.cloned.1.call-start = ((), (), s32[]{:S(2)}) async-start(), calls=%async_computation.2 | async-start | bytes 8912896 | tf_op jit(solution)/shard_map/all_gather | solution.py:74
  9.1 173.9 %all-gather.9.cloned.1.call-start = ((), (), s32[]{:S(2)}) async-start(), calls=%async_computation.3 | async-start | bytes 4456448 | tf_op jit(solution)/shard_map/all_gather | solution.py:91
  55.5 3.2 %copy-start.1 = (f32[2,2048,64,8]{1,2,3,0:T(8,128)}, f32[2,2048,64,8]{1,2,3,0:T(8,128)S(1)}, u32[]{:S(2)}) copy-start(f32[2,2048,64,8]{1,2,3,0:T(8,128)S(1)} %get-tuple-element.34) | copy-start | bytes 25165828
  58.9 5.7 %copy-start.3 = (bf16[64,2,8,64]{3,2,0,1:T(8,128)(2,1)S(1)}, bf16[64,2,8,64]{3,2,0,1:T(8,128)(2,1)}, u32[]{:S(2)}) copy-start(bf16[64,2,8,64]{3,2,0,1:T(8,128)(2,1)} %copy.67) | copy-start | bytes 393220
  126.4 5.9 %copy-start.4 = (f32[2048]{0:T(1024)S(1)}, f32[2048]{0:T(1024)}, u32[]{:S(2)}) copy-start(f32[2048]{0:T(1024)} %param.18) | copy-start | bytes 24580
  126.4 6.8 %copy-start.8 = (s32[16]{0:T(128)S(1)}, s32[16]{0:T(128)}, u32[]{:S(2)}) copy-start(s32[16]{0:T(128)} %param.22) | copy-start | bytes 196
  126.4 7.0 %copy-start.5 = (f32[64,8]{0,1:T(8,128)S(1)}, f32[64,8]{0,1:T(8,128)}, u32[]{:S(2)}) copy-start(f32[64,8]{0,1:T(8,128)} %param.21) | copy-start | bytes 6148
  126.4 7.0 %copy-start.6 = (s32[64,8]{0,1:T(8,128)S(1)}, s32[64,8]{0,1:T(8,128)}, u32[]{:S(2)}) copy-start(s32[64,8]{0,1:T(8,128)} %param.20) | copy-start | bytes 6148
  126.4 7.0 %copy-start.7 = (s32[64,8]{0,1:T(8,128)S(1)}, s32[64,8]{0,1:T(8,128)}, u32[]{:S(2)}) copy-start(s32[64,8]{0,1:T(8,128)} %param.19) | copy-start | bytes 6148
  131.5 0.8 copy-start.2
  133.2 142.2 %reduce-scatter.2.cloned.1.call-start = ((), (), s32[]{:S(2)}) async-start(), calls=%async_computation.4 | async-start | bytes 4456448 | tf_op jit(solution)/shard_map/reduce_scatter | solution.py:97
Sparse Core Ops, SparseCore 0:
  9.5 41.8 all-gather.4
  53.6 72.7 all-gather.6
  133.3 49.6 all-gather.8
  203.7 71.6 reduce-scatter.1

commit v2 on v1

--- a/solution.py
+++ b/solution.py
@@ -1,14 +1,306 @@
+import functools
 import math
 
 import jax
 import jax.numpy as jnp
 from jax import lax
+from jax.experimental import pallas as pl
+from jax.experimental.pallas import tpu as pltpu
 from jax.sharding import PartitionSpec as P
 
 QUERY_HEADS = 16
 KEY_VALUE_HEADS = 2
 HEAD_SIZE = 128
 QLEN = 16
+
+
+MESH = pl.DeviceIdType.MESH
+PLANE = 4
+
+
+def place(levels):
+    line = lax.axis_index("line")
+    group = lax.axis_index("group")
+    level, side, core = line // PLANE, (line // 2) % 2, line % 2
+
+    def device(level, side, core):
+        return (group, level * PLANE + side * 2 + core)
+
+    barrier = pltpu.get_barrier_semaphore()
+    has_up, has_down = level + 1 < levels, level > 0
+
+    def greet(target):
+        pl.semaphore_signal(barrier, inc=1, device_id=target, device_id_type=MESH)
+
+    greet(device(level, 1 - side, core))
+    greet(device(level, side, 1 - core))
+    pl.when(has_up)(lambda: greet(device(level + 1, side, core)))
+    pl.when(has_down)(lambda: greet(device(level - 1, side, core)))
+    inner = has_up & has_down
+    pl.when(inner)(lambda: pl.semaphore_wait(barrier, 4))
+    pl.when(jnp.logical_not(inner))(lambda: pl.semaphore_wait(barrier, 3))
+    return level, side, core, device, has_up, has_down
+
+
+def run_if(condition, action):
+    if condition is None:
+        action()
+    else:
+        pl.when(condition)(action)
+
+
+def both(first, second):
+    return second if first is None else first & second
+
+
+def gather_kernel(levels, arrays, *refs):
+    ins, outs = refs[:arrays], refs[arrays : 2 * arrays]
+    up_sem, down_sem, side_sem, core_sem, recv_sem, own_sem = refs[2 * arrays :]
+    level, side, core, device, has_up, has_down = place(levels)
+    above, below = device(level + 1, side, core), device(level - 1, side, core)
+    across, twin = device(level, 1 - side, core), device(level, side, 1 - core)
+    pending = []
+
+    def slot_of(at_level, at_side, at_core):
+        return at_level * PLANE + at_side * 2 + at_core
+
+    def send(array, slot, source, target, sem, condition):
+        copy = pltpu.make_async_remote_copy(
+            src_ref=source,
+            dst_ref=outs[array].at[slot],
+            send_sem=sem,
+            recv_sem=recv_sem.at[array, slot],
+            device_id=target,
+            device_id_type=MESH,
+        )
+        run_if(condition, copy.start)
+        pending.append((condition, copy))
+
+    def arrived(array, slot, condition):
+        copy = pltpu.make_async_remote_copy(
+            src_ref=outs[array].at[slot],
+            dst_ref=outs[array].at[slot],
+            send_sem=own_sem.at[array],
+            recv_sem=recv_sem.at[array, slot],
+            device_id=twin,
+            device_id_type=MESH,
+        )
+        run_if(condition, copy.wait_recv)
+
+    mine = slot_of(level, side, core)
+    own = []
+    for array in range(arrays):
+        source = ins[array]
+        send(array, mine, source, above, up_sem.at[array, 0], has_up)
+        send(array, mine, source, below, down_sem.at[array, 0], has_down)
+        send(array, mine, source, across, side_sem.at[array, 0], None)
+        send(array, mine, source, twin, core_sem.at[array, 0], None)
+        copy = pltpu.make_async_copy(source, outs[array].at[mine], own_sem.at[array])
+        copy.start()
+        own.append(copy)
+    for hop in range(1, levels):
+        for array in range(arrays):
+            there = level - hop >= 0
+            slot = slot_of(level - hop, side, core)
+            source = outs[array].at[slot]
+            arrived(array, slot, there)
+            send(array, slot, source, above, up_sem.at[array, hop], there & has_up)
+            send(array, slot, source, across, side_sem.at[array, 2 * hop - 1], there)
+            send(array, slot, source, twin, core_sem.at[array, 2 * hop - 1], there)
+            there = level + hop < levels
+            slot = slot_of(level + hop, side, core)
+            source = outs[array].at[slot]
+            arrived(array, slot, there)
+            send(array, slot, source, below, down_sem.at[array, hop], there & has_down)
+            send(array, slot, source, across, side_sem.at[array, 2 * hop], there)
+            send(array, slot, source, twin, core_sem.at[array, 2 * hop], there)
+    base = 2 * levels
+    for hop in range(levels):
+        for array in range(arrays):
+            for sign in (-1, 1) if hop else (1,):
+                at_level = level + sign * hop
+                there = (at_level >= 0) & (at_level < levels) if hop else None
+                slot = slot_of(at_level, 1 - side, core)
+                arrived(array, slot, there)
+                index = base + 2 * hop + (sign + 1) // 2
+                send(array, slot, outs[array].at[slot], twin, core_sem.at[array, index], there)
+    for array in range(arrays):
+        for at_level in range(levels):
+            for at_side in range(2):
+                arrived(array, slot_of(at_level, at_side, 1 - core), None)
+        own[array].wait()
+    for condition, copy in pending:
+        run_if(condition, copy.wait_send)
+
+
+def gather(levels, identity, *arrays):
+    count = len(arrays)
+    devices = levels * PLANE
+    sem = pltpu.SemaphoreType.DMA
+    anywhere = pl.BlockSpec(memory_space=pl.ANY)
+    outs = pl.pallas_call(
+        functools.partial(gather_kernel, levels, count),
+        out_shape=[jax.ShapeDtypeStruct((devices,) + a.shape, a.dtype) for a in arrays],
+        in_specs=[anywhere] * count,
+        out_specs=[anywhere] * count,
+        scratch_shapes=[
+            sem((count, levels)),
+            sem((count, levels)),
+            sem((count, 2 * levels)),
+            sem((count, 4 * levels)),
+            sem((count, devices)),
+            sem((count,)),
+        ],
+        compiler_params=pltpu.CompilerParams(collective_id=identity, has_side_effects=True),
+    )(*arrays)
+    return [out.reshape((-1, out.shape[-1])) for out in outs]
+
+
+def scatter_kernel(
+    levels,
+    share,
+    out,
+    core_in,
+    side_in,
+    up_in,
+    down_in,
+    side_out,
+    z_out,
+    core_send,
+    core_recv,
+    side_send,
+    side_recv,
+    z_send,
+    up_recv,
+    down_recv,
+):
+    level, side, core, device, has_up, has_down = place(levels)
+    above, below = device(level + 1, side, core), device(level - 1, side, core)
+    across, twin = device(level, 1 - side, core), device(level, side, 1 - core)
+    wide = jnp.float32
+
+    def copy(source, landing, sem, recv, target):
+        return pltpu.make_async_remote_copy(
+            src_ref=source,
+            dst_ref=landing,
+            send_sem=sem,
+            recv_sem=recv,
+            device_id=target,
+            device_id_type=MESH,
+        )
+
+    order = []
+    for step in range(levels // 2):
+        order += [levels - 1 - step, step]
+    pending = []
+    core_copies = {}
+    for far in (1, 0):
+        for at in order:
+            at_side = 1 - side if far else side
+            block = share.at[at * PLANE + at_side * 2 + (1 - core)]
+            index = at * 2 + far
+            one = copy(
+                block, core_in.at[index], core_send.at[index], core_recv.at[index], twin
+            )
+            one.start()
+            pending.append((None, one))
+            core_copies[index] = one
+    side_copies = {}
+    for at in order:
+        core_copies[at * 2 + 1].wait_recv()
+        slot = at * PLANE + (1 - side) * 2 + core
+        side_out[at] = (share[slot].astype(wide) + core_in[at * 2 + 1].astype(wide)).astype(
+            side_out.dtype
+        )
+        one = copy(side_out.at[at], side_in.at[at], side_send.at[at], side_recv.at[at], across)
+        one.start()
+        pending.append((None, one))
+        side_copies[at] = one
+    for at in order:
+        core_copies[at * 2].wait_recv()
+        side_copies[at].wait_recv()
+        up = copy(z_out.at[at], up_in.at[at], z_send.at[at], up_recv.at[at], above)
+        down = copy(z_out.at[at], down_in.at[at], z_send.at[at], down_recv.at[at], below)
+
+        def local(at=at):
+            slot = at * PLANE + side * 2 + core
+            return (
+                share[slot].astype(wide)
+                + core_in[at * 2].astype(wide)
+                + side_in[at].astype(wide)
+            )
+
+        def start(value, one, at=at):
+            z_out[at] = value.astype(z_out.dtype)
+            one.start()
+
+        def climb(at=at, up=up, local=local, start=start):
+            up.wait_recv()
+            start(local() + up_in[at].astype(wide), up)
+
+        def drop(at=at, down=down, local=local, start=start):
+            down.wait_recv()
+            start(local() + down_in[at].astype(wide), down)
+
+        def keep(local=local):
+            out[...] = local()
+
+        pl.when((at > level) & has_down)(climb)
+        pl.when((at > level) & (level == 0))(lambda: start(local(), up))
+        pl.when((at < level) & has_up)(drop)
+        pl.when((at < level) & (level == levels - 1))(lambda: start(local(), down))
+        pl.when(at == level)(keep)
+        pending.append((at > level, up))
+        pending.append((at < level, down))
+
+    for at in range(levels):
+        up = copy(z_out.at[at], up_in.at[at], z_send.at[at], up_recv.at[at], above)
+        down = copy(z_out.at[at], down_in.at[at], z_send.at[at], down_recv.at[at], below)
+
+        def take_up(at=at, up=up):
+            up.wait_recv()
+            out[...] += up_in[at].astype(wide)
+
+        def take_down(at=at, down=down):
+            down.wait_recv()
+            out[...] += down_in[at].astype(wide)
+
+        pl.when((at == level) & has_down)(take_up)
+        pl.when((at == level) & has_up)(take_down)
+    for condition, one in pending:
+        run_if(condition, one.wait_send)
+
+
+def scatter(levels, identity, share):
+    devices = levels * PLANE
+    rows, width = share.shape[0] // devices, share.shape[1]
+    sem = pltpu.SemaphoreType.DMA
+    block = (rows, width)
+    vmem = pl.BlockSpec(memory_space=pltpu.VMEM)
+    return pl.pallas_call(
+        functools.partial(scatter_kernel, levels),
+        out_shape=jax.ShapeDtypeStruct(block, jnp.float32),
+        in_specs=[vmem],
+        out_specs=vmem,
+        scratch_shapes=[
+            pltpu.VMEM((2 * levels,) + block, share.dtype),
+            pltpu.VMEM((levels,) + block, share.dtype),
+            pltpu.VMEM((levels,) + block, share.dtype),
+            pltpu.VMEM((levels,) + block, share.dtype),
+            pltpu.VMEM((levels,) + block, share.dtype),
+            pltpu.VMEM((levels,) + block, share.dtype),
+            sem((2 * levels,)),
+            sem((2 * levels,)),
+            sem((levels,)),
+            sem((levels,)),
+            sem((levels,)),
+            sem((levels,)),
+            sem((levels,)),
+        ],
+        compiler_params=pltpu.CompilerParams(
+            collective_id=identity, has_side_effects=True, vmem_limit_bytes=40 * 1024 * 1024
+        ),
+    )(share.reshape((devices,) + block))
 
 
 def attention(queries, local_kv, prefix):
@@ -70,8 +362,9 @@
     expert_up,
     expert_down,
 ):
-    prefix = lax.all_gather(document_prefix_cache, "line", axis=0, tiled=True)
-    projection = lax.all_gather(out_proj, "line", axis=0, tiled=True)
+    count = lax.axis_size("line")
+    small = count % (2 * PLANE) == 0 and count * queries.shape[0] <= 2048
+    levels = count // PLANE
     numbers = jnp.arange(expert_slots.shape[0], dtype=jnp.int32)
     slot_of_number = expert_slots[None, :] == numbers[:, None]
     number_of_slot = jnp.sum(jnp.where(slot_of_number, numbers[None, :], 0), axis=1)
@@ -80,7 +373,15 @@
         jnp.where(routes[:, :, None] == number_of_slot[None, None, :], kept[:, :, None], 0.0),
         axis=1,
     )
-    all_slots = lax.all_gather(per_slot, "line", axis=0, tiled=True)
+    if small:
+        per_slot = jnp.pad(per_slot, ((0, 0), (0, -per_slot.shape[1] % 128)))
+        prefix, projection, all_slots = gather(
+            levels, 0, document_prefix_cache, out_proj, per_slot
+        )
+    else:
+        prefix = lax.all_gather(document_prefix_cache, "line", axis=0, tiled=True)
+        projection = lax.all_gather(out_proj, "line", axis=0, tiled=True)
+        all_slots = lax.all_gather(per_slot, "line", axis=0, tiled=True)
     weight = lax.dynamic_slice_in_dim(all_slots, lax.axis_index("line"), 1, 1)
     context = attention(queries, question_key_values, prefix)
     attended = jnp.dot(context, projection, preferred_element_type=jnp.float32)
@@ -88,13 +389,19 @@
     normed = (
         mixture * lax.rsqrt(jnp.mean(mixture * mixture, axis=-1, keepdims=True) + 1e-06) * norm_gain
     ).astype(jnp.bfloat16)
-    rows = lax.all_gather(normed, "line", axis=0, tiled=True)
+    if small:
+        (rows,) = gather(levels, 1, normed)
+    else:
+        rows = lax.all_gather(normed, "line", axis=0, tiled=True)
     gate = jnp.dot(rows, expert_gate[0], preferred_element_type=jnp.float32)
     upper = jnp.dot(rows, expert_up[0], preferred_element_type=jnp.float32)
     middle = (jax.nn.silu(gate) * upper).astype(jnp.bfloat16)
     answer = jnp.dot(middle, expert_down[0], preferred_element_type=jnp.float32)
     share = (answer.astype(jnp.bfloat16).astype(jnp.float32) * weight).astype(jnp.bfloat16)
-    summed = lax.psum_scatter(share, "line", scatter_dimension=0, tiled=True)
+    if small:
+        summed = scatter(levels, 2, share)
+    else:
+        summed = lax.psum_scatter(share, "line", scatter_dimension=0, tiled=True)
     return (mixture + summed.astype(jnp.float32)).astype(jnp.bfloat16)
 
 

time: 286 us -> 198 us (0.69)
  waiting for transfers between devices: 203 us -> 0 us
  Pallas kernels: 0 us -> 138 us
  blocking collectives: 17 us -> 0 us
  between operations: 13.3 us -> 0.16 us
  local copies, waits for them, and re-layouts: 10.8 us -> 19 us
    pallas_call x0 -> x3, Pallas kernels: none -> 138 us  [the longest x2 95 us: gather(): pl.pallas_call(functools.partial(gather_kernel, levels, count), out_shape...]
    all_gather x3 -> x0, waiting for transfers between devices: 131 us -> none  [the longest x1 61.3 us: body(): projection = lax.all_gather(out_proj, 'line', axis=0, tiled=True)]
    reduce_scatter x1 -> x0, waiting for transfers between devices: 71.8 us -> none  [body(): summed = lax.psum_scatter(share, 'line', scatter_dimension=0, tiled=True)]
    all_gather x1 -> x0, blocking collectives: 17 us -> none  [body(): all_slots = lax.all_gather(per_slot, 'line', axis=0, tiled=True)]
    unnamed x21 -> x18, local copies, waits for them, and re-layouts: 5.22 us -> 9.81 us
  transfers between devices with their start and end apart: 4 -> 0, of which waited for: 4 -> 0; matrix products, arithmetic and copies ran while one was open for 6% -> 0% of each run, Pallas kernels for 0% -> 0%
where the time goes in v2:
time: 198 us
  Pallas kernels  138 us (70%)
  matrix products  33.5 us (17%)
  local copies, waits for them, and re-layouts  19 us (10%)
  other arithmetic  6.73 us (3%)
    pallas_call x2, Pallas kernels, gather(): pl.pallas_call(functools.partial(gather_kernel, levels, count), out_shape...  95 us
    pallas_call x1, Pallas kernels, scatter(): pl.pallas_call(functools.partial(scatter_kernel, levels), out_shape=jax.S...  43.5 us
    dot_general x1, matrix products, body(): answer = jnp.dot(middle, expert_down[0], preferred_element_type=jnp.float32)  12.3 us
    unnamed x18, local copies, waits for them, and re-layouts  9.81 us
    dot_general x1, matrix products, body(): upper = jnp.dot(rows, expert_up[0], preferred_element_type=jnp.float32)  8.33 us
    dot_general x1, matrix products, body(): attended = jnp.dot(context, projection, preferred_element_type=jnp.float32)  5.08 us

profile of v2, /device:TPU:10, one launch (start us, length us, event | category | flops | bytes accessed | tf_op | source)
XLA Modules:
  0.0 197.8 jit_solution(1048098262668731261)
XLA Ops:
  0.0 0.0 copy-start
  0.0 0.9 select_reduce_fusion.1
  0.9 0.7 compare_select_fusion
  1.7 0.8 select_reduce_fusion
  2.4 0.1 fusion.32
  2.5 0.1 copy.42
  2.6 0.6 pad.4.refs_2_
  3.2 0.8 fusion.35
  4.0 0.6 reshape.178
  4.6 1.0 copy.68
  5.6 0.4 fusion.36
  6.0 0.8 fusion.23
  6.8 1.8 copy.40
  8.7 64.8 %shard_map.127 = (bf16[16,128,512]{2,1,0:T(8,128)(2,1)}, bf16[16,128,2048]{2,1,0:T(8,128)(2,1)}, f32[16,64,128]{2,1,0:T(8,128)}) custom-call(bf16[128,512]{1,0:T(8,128)(2,1)} %refs_0_.1, bf16[128,2048]{1,0:T(8,128)(2,1)} %refs_1_.1, f32[64,128]{1,0:T(8,128)} %pad.4.refs_2_), custom_call_target="tpu_custom_call" | custom-call | tf_op jit(solution)/shard_map/pallas_call | solution.py:141
  73.5 3.0 %fusion.34 = (bf16[2048,256]{1,0:T(8,128)(2,1)}, bf16[2048,256]{1,0:T(8,128)(2,1)}) fusion(bf16[2048,512]{1,0:T(8,128)(2,1)} %bitcast.79), kind=kLoop, calls=%fused_computation.52 | loop fusion | bytes 4194304 | tf_op jit(solution)/shard_map/while/body/eval_jaxpr/slice | solution.py:333
  76.4 2.3 %copy.65 = bf16[2048,256]{0,1:T(8,128)(2,1)} copy(bf16[2048,256]{1,0:T(8,128)(2,1)} %get-tuple-element.33) | data formatting | bytes 2097152
  78.8 2.0 %constant_dynamic-slice_fusion = f32[1024,1]{1,0:T(8,128)} fusion(f32[1024,128]{1,0:T(8,128)} %bitcast.82, s32[]{:T(128)S(6)} %select_n.42), kind=kLoop, calls=%fused_computation.50 | loop fusion | bytes 8196 | tf_op jit(solution)/shard_map/dynamic_slice | solution.py:385
  80.8 1.2 copy.67
  82.0 2.3 %copy.66 = bf16[2048,256]{0,1:T(8,128)(2,1)} copy(bf16[2048,256]{1,0:T(8,128)(2,1)} %get-tuple-element.34) | data formatting | bytes 2097152
  84.3 2.5 %bitcast_reduce_fusion = (f32[64,2,8]{0,2,1:T(8,128)S(1)}, f32[2,2048,64,8]{1,2,3,0:T(8,128)S(1)}) fusion(bf16[2048,2,128,1]{0,2,3,1:T(8,128)(2,1)} %bitcast.74, bf16[64,2,8,128]{3,2,1,0:T(8,128)(2,1)S(1)} %bitcast.78), kind=kOutput, calls=%fused_computation.1 | convolution fusion | flops 541064192 | bytes 9703424 | tf_op jit(solution)/shard_map/while/body/eval_jaxpr/thgd,nhd->thgn/dot_general | solution.py:335
  86.9 0.0 copy-start.4
  86.9 1.8 fusion.1
  88.7 0.0 copy-done.4
  88.7 0.0 copy-start.5
  88.7 3.3 %fusion.12 = f32[64,2,8,128]{3,2,0,1:T(8,128)} fusion(bf16[2048,2,128,1]{0,2,3,1:T(8,128)(2,1)S(1)} %bitcast.81, bf16[64,2,8,2048]{3,0,2,1:T(8,128)(2,1)S(1)} %get-tuple-element.32), kind=kOutput, calls=%fused_computation.15 | convolution fusion | flops 536870912 | bytes 5767168 | tf_op jit(solution)/shard_map/while/body/eval_jaxpr/thgn,nhd->thgd/dot_general | solution.py:339
  92.0 0.1 copy.50
  92.1 0.1 copy.46
  92.2 1.5 fusion.20
  93.7 0.0 copy-done.5
  93.8 0.0 copy-start.6
  93.8 5.1 %multiply_reduce_fusion = (f32[64]{0:T(128)S(1)}, f32[64,2048]{1,0:T(8,128)S(1)}) fusion(bf16[2048,2048]{1,0:T(8,128)(2,1)} %bitcast.73, bf16[8,8,16,128]{3,2,1,0:T(8,128)(2,1)S(1)} %bitcast.80, bf16[64,2048]{1,0:T(8,128)(2,1)S(1)} %copy-done.5), kind=kOutput, calls=%fused_computation.26 | convolution fusion | flops 537395136 | bytes 9437440 | tf_op jit(solution)/shard_map/dot_general | solution.py:387
  98.9 0.0 copy-start.2
  98.9 0.8 copy-done.2
  99.7 0.0 copy-done.6
  99.7 0.8 multiply_convert_fusion.2.refs_0_
  100.5 30.2 %shard_map.128 = bf16[16,64,2048]{2,1,0:T(8,128)(2,1)} custom-call(bf16[64,2048]{1,0:T(8,128)(2,1)} %multiply_convert_fusion.2.refs_0_), custom_call_target="tpu_custom_call" | custom-call | tf_op jit(solution)/shard_map/pallas_call | solution.py:141
  130.7 8.3 %fusion.6 = f32[1024,768]{1,0:T(8,128)} fusion(bf16[1024,2048]{1,0:T(8,128)(2,1)} %bitcast.75, bf16[1,2048,768]{2,1,0:T(8,128)(2,1)} %param.24), kind=kOutput, calls=%fused_computation.9 | convolution fusion | flops 3221225472 | bytes 10485760 | tf_op jit(solution)/shard_map/dot_general | solution.py:397
  139.0 0.0 copy-done
  139.0 12.3 %multiply_convert_fusion = bf16[1024,2048]{1,0:T(8,128)(2,1)} fusion(f32[1024]{0:T(1024)S(1)} %bitcast.86, bf16[1,768,2048]{2,1,0:T(8,128)(2,1)S(1)} %copy-done, f32[1024,768]{1,0:T(8,128)} %fusion.6, bf16[1024,2048]{1,0:T(8,128)(2,1)} %bitcast.76, bf16[1,2048,768]{2,1,0:T(8,128)(2,1)} %param.23), kind=kOutput, calls=%fused_computation.3 | convolution fusion | flops 6455558144 | bytes 17829888 | tf_op jit(solution)/shard_map/dot_general | solution.py:399
  151.4 0.0 copy-start.1
  151.4 2.2 %copy-done.1 = bf16[1024,2048]{1,0:T(8,128)(2,1)S(1)} copy-done((bf16[1024,2048]{1,0:T(8,128)(2,1)S(1)}, bf16[1024,2048]{1,0:T(8,128)(2,1)}, u32[]{:S(2)}) %copy-start.1) | copy-done | bytes 4194328
  153.6 0.0 copy-start.3
  153.6 43.5 %shard_map.129 = f32[64,2048]{1,0:T(8,128)S(1)} custom-call(bf16[16,64,2048]{2,1,0:T(8,128)(2,1)S(1)} %bitcast.72), custom_call_target="tpu_custom_call" | custom-call | tf_op jit(solution)/shard_map/pallas_call | solution.py:280
  197.0 0.0 copy-done.3
  197.1 0.8 add_convert_fusion
  (6 shorter events, 0.1 us)
Async XLA Ops:
  0.0 139.0 %copy-start = (bf16[1,768,2048]{2,1,0:T(8,128)(2,1)S(1)}, bf16[1,768,2048]{2,1,0:T(8,128)(2,1)}, u32[]{:S(2)}) copy-start(bf16[1,768,2048]{2,1,0:T(8,128)(2,1)} %param.25) | copy-start | bytes 9437188
  86.9 1.8 copy-start.4
  88.7 5.1 %copy-start.5 = (bf16[64,2048]{1,0:T(8,128)(2,1)S(1)}, bf16[64,2048]{1,0:T(8,128)(2,1)}, u32[]{:S(2)}) copy-start(bf16[64,2048]{1,0:T(8,128)(2,1)} %param.13) | copy-start | bytes 786436
  93.8 5.9 %copy-start.6 = (f32[2048]{0:T(1024)S(1)}, f32[2048]{0:T(1024)}, u32[]{:S(2)}) copy-start(f32[2048]{0:T(1024)} %param.18) | copy-start | bytes 24580
  98.9 0.8 copy-start.2
  151.4 2.2 %copy-start.1 = (bf16[1024,2048]{1,0:T(8,128)(2,1)S(1)}, bf16[1024,2048]{1,0:T(8,128)(2,1)}, u32[]{:S(2)}) copy-start(bf16[1024,2048]{1,0:T(8,128)(2,1)} %multiply_convert_fusion) | copy-start | bytes 12582916
  153.6 43.5 %copy-start.3 = (f32[64,2048]{1,0:T(8,128)S(1)}, f32[64,2048]{1,0:T(8,128)}, u32[]{:S(2)}) copy-start(f32[64,2048]{1,0:T(8,128)} %copy-done.2) | copy-start | bytes 1572868

commit v3 on v2

--- a/solution.py
+++ b/solution.py
@@ -18,7 +18,7 @@
 PLANE = 4
 
 
-def place(levels):
+def place(levels, pair=False):
     line = lax.axis_index("line")
     group = lax.axis_index("group")
     level, side, core = line // PLANE, (line // 2) % 2, line % 2
@@ -32,13 +32,16 @@
     def greet(target):
         pl.semaphore_signal(barrier, inc=1, device_id=target, device_id_type=MESH)
 
+    if pair:
+        greet((1 - group, line))
+    extra = 1 if pair else 0
     greet(device(level, 1 - side, core))
     greet(device(level, side, 1 - core))
     pl.when(has_up)(lambda: greet(device(level + 1, side, core)))
     pl.when(has_down)(lambda: greet(device(level - 1, side, core)))
     inner = has_up & has_down
-    pl.when(inner)(lambda: pl.semaphore_wait(barrier, 4))
-    pl.when(jnp.logical_not(inner))(lambda: pl.semaphore_wait(barrier, 3))
+    pl.when(inner)(lambda: pl.semaphore_wait(barrier, 4 + extra))
+    pl.when(jnp.logical_not(inner))(lambda: pl.semaphore_wait(barrier, 3 + extra))
     return level, side, core, device, has_up, has_down
 
 
@@ -53,10 +56,13 @@
     return second if first is None else first & second
 
 
-def gather_kernel(levels, arrays, *refs):
+def gather_kernel(levels, arrays, shared, *refs):
     ins, outs = refs[:arrays], refs[arrays : 2 * arrays]
-    up_sem, down_sem, side_sem, core_sem, recv_sem, own_sem = refs[2 * arrays :]
-    level, side, core, device, has_up, has_down = place(levels)
+    up_sem, down_sem, side_sem, core_sem, recv_sem, own_sem = refs[2 * arrays : 2 * arrays + 6]
+    pair_send, pair_core, pair_recv = refs[2 * arrays + 6 :]
+    level, side, core, device, has_up, has_down = place(levels, shared is not None)
+    group = lax.axis_index("group")
+    peer = (1 - group, lax.axis_index("line"))
     above, below = device(level + 1, side, core), device(level - 1, side, core)
     across, twin = device(level, 1 - side, core), device(level, side, 1 - core)
     pending = []
@@ -64,24 +70,34 @@
     def slot_of(at_level, at_side, at_core):
         return at_level * PLANE + at_side * 2 + at_core
 
-    def send(array, slot, source, target, sem, condition):
+    def part_of(array, ref, which):
+        if which is None:
+            return ref
+        half = ins[array].shape[0] // 2
+        return ref.at[pl.ds(pl.multiple_of(which * half, half), half)]
+
+    def send(array, slot, source, target, sem, condition, which=None, recv=None):
         copy = pltpu.make_async_remote_copy(
-            src_ref=source,
-            dst_ref=outs[array].at[slot],
+            src_ref=part_of(array, source, which),
+            dst_ref=part_of(array, outs[array].at[slot], which),
             send_sem=sem,
-            recv_sem=recv_sem.at[array, slot],
+            recv_sem=recv_sem.at[array, slot] if recv is None else recv,
             device_id=target,
             device_id_type=MESH,
         )
         run_if(condition, copy.start)
         pending.append((condition, copy))
 
-    def arrived(array, slot, condition):
+    def half_of(array):
+        return group if array == shared else None
+
+    def arrived(array, slot, condition, which=None, recv=None):
+        landing = part_of(array, outs[array].at[slot], which)
         copy = pltpu.make_async_remote_copy(
-            src_ref=outs[array].at[slot],
-            dst_ref=outs[array].at[slot],
+            src_ref=landing,
+            dst_ref=landing,
             send_sem=own_sem.at[array],
-            recv_sem=recv_sem.at[array, slot],
+            recv_sem=recv_sem.at[array, slot] if recv is None else recv,
             device_id=twin,
             device_id_type=MESH,
         )
@@ -93,7 +109,7 @@
         source = ins[array]
         send(array, mine, source, above, up_sem.at[array, 0], has_up)
         send(array, mine, source, below, down_sem.at[array, 0], has_down)
-        send(array, mine, source, across, side_sem.at[array, 0], None)
+        send(array, mine, source, across, side_sem.at[array, 0], None, half_of(array))
         send(array, mine, source, twin, core_sem.at[array, 0], None)
         copy = pltpu.make_async_copy(source, outs[array].at[mine], own_sem.at[array])
         copy.start()
@@ -105,41 +121,67 @@
             source = outs[array].at[slot]
             arrived(array, slot, there)
             send(array, slot, source, above, up_sem.at[array, hop], there & has_up)
-            send(array, slot, source, across, side_sem.at[array, 2 * hop - 1], there)
+            send(array, slot, source, across, side_sem.at[array, 2 * hop - 1], there, half_of(array))
             send(array, slot, source, twin, core_sem.at[array, 2 * hop - 1], there)
             there = level + hop < levels
             slot = slot_of(level + hop, side, core)
             source = outs[array].at[slot]
             arrived(array, slot, there)
             send(array, slot, source, below, down_sem.at[array, hop], there & has_down)
-            send(array, slot, source, across, side_sem.at[array, 2 * hop], there)
+            send(array, slot, source, across, side_sem.at[array, 2 * hop], there, half_of(array))
             send(array, slot, source, twin, core_sem.at[array, 2 * hop], there)
     base = 2 * levels
-    for hop in range(levels):
-        for array in range(arrays):
-            for sign in (-1, 1) if hop else (1,):
-                at_level = level + sign * hop
-                there = (at_level >= 0) & (at_level < levels) if hop else None
-                slot = slot_of(at_level, 1 - side, core)
-                arrived(array, slot, there)
-                index = base + 2 * hop + (sign + 1) // 2
-                send(array, slot, outs[array].at[slot], twin, core_sem.at[array, index], there)
+    for stage in range(2):
+        for hop in range(levels):
+            for array in range(arrays):
+                if stage == 1 and array != shared:
+                    continue
+                for sign in (-1, 1) if hop else (1,):
+                    at_level = level + sign * hop
+                    there = (at_level >= 0) & (at_level < levels) if hop else None
+                    slot = slot_of(at_level, 1 - side, core)
+                    index = 2 * hop + (sign + 1) // 2
+                    source = outs[array].at[slot]
+                    if stage == 0:
+                        half = half_of(array)
+                        arrived(array, slot, there, half)
+                        if array == shared:
+                            send(
+                                array,
+                                slot,
+                                source,
+                                peer,
+                                pair_send.at[index],
+                                there,
+                                half,
+                                pair_recv.at[slot],
+                            )
+                        sem = core_sem.at[array, base + index]
+                        send(array, slot, source, twin, sem, there, half)
+                    else:
+                        half = 1 - group
+                        arrived(array, slot, there, half, pair_recv.at[slot])
+                        sem = pair_core.at[index]
+                        send(array, slot, source, twin, sem, there, half, pair_recv.at[slot])
     for array in range(arrays):
         for at_level in range(levels):
-            for at_side in range(2):
-                arrived(array, slot_of(at_level, at_side, 1 - core), None)
+            arrived(array, slot_of(at_level, side, 1 - core), None)
+            slot = slot_of(at_level, 1 - side, 1 - core)
+            arrived(array, slot, None, half_of(array))
+            if array == shared:
+                arrived(array, slot, None, 1 - group, pair_recv.at[slot])
         own[array].wait()
     for condition, copy in pending:
         run_if(condition, copy.wait_send)
 
 
-def gather(levels, identity, *arrays):
+def gather(levels, identity, *arrays, shared=None):
     count = len(arrays)
     devices = levels * PLANE
     sem = pltpu.SemaphoreType.DMA
     anywhere = pl.BlockSpec(memory_space=pl.ANY)
     outs = pl.pallas_call(
-        functools.partial(gather_kernel, levels, count),
+        functools.partial(gather_kernel, levels, count, shared),
         out_shape=[jax.ShapeDtypeStruct((devices,) + a.shape, a.dtype) for a in arrays],
         in_specs=[anywhere] * count,
         out_specs=[anywhere] * count,
@@ -150,6 +192,9 @@
             sem((count, 4 * levels)),
             sem((count, devices)),
             sem((count,)),
+            sem((2 * levels,)),
+            sem((2 * levels,)),
+            sem((devices,)),
         ],
         compiler_params=pltpu.CompilerParams(collective_id=identity, has_side_effects=True),
     )(*arrays)
@@ -303,6 +348,82 @@
     )(share.reshape((devices,) + block))
 
 
+def attend_kernel(q_ref, key_ref, value_ref, near_key_ref, near_value_ref, out_ref):
+    tokens = q_ref.shape[0]
+    heads = q_ref.shape[1] // HEAD_SIZE
+    scale = 1.0 / math.sqrt(HEAD_SIZE)
+    q = jnp.concatenate(
+        [q_ref[:, i * HEAD_SIZE : (i + 1) * HEAD_SIZE] for i in range(heads)], axis=0
+    )
+    dims = (((1,), (1,)), ((), ()))
+    far = lax.dot_general(q, key_ref[...], dims, preferred_element_type=jnp.float32) * scale
+    near = lax.dot_general(q, near_key_ref[...], dims, preferred_element_type=jnp.float32) * scale
+    token = lax.rem(lax.broadcasted_iota(jnp.int32, near.shape, 0), tokens)
+    other = lax.broadcasted_iota(jnp.int32, near.shape, 1)
+    near = jnp.where((token // QLEN == other // QLEN) & (other <= token), near, -1e30)
+    top = jnp.maximum(far.max(-1, keepdims=True), near.max(-1, keepdims=True))
+    far = jnp.exp(far - top)
+    near = jnp.exp(near - top)
+    total = far.sum(-1, keepdims=True) + near.sum(-1, keepdims=True)
+    acc = jnp.dot(far.astype(jnp.bfloat16), value_ref[...], preferred_element_type=jnp.float32)
+    acc += jnp.dot(
+        near.astype(jnp.bfloat16), near_value_ref[...], preferred_element_type=jnp.float32
+    )
+    context = (acc / total).astype(out_ref.dtype)
+    for i in range(heads):
+        out_ref[:, i * HEAD_SIZE : (i + 1) * HEAD_SIZE] = context[i * tokens : (i + 1) * tokens]
+
+
+def attend(queries, local_kv, prefix):
+    tokens, rows = queries.shape[0], prefix.shape[0]
+    wide = 4 * HEAD_SIZE
+    steps = QUERY_HEADS // KEY_VALUE_HEADS // 4
+    return pl.pallas_call(
+        attend_kernel,
+        grid=(KEY_VALUE_HEADS, steps),
+        out_shape=jax.ShapeDtypeStruct(queries.shape, queries.dtype),
+        in_specs=[
+            pl.BlockSpec((tokens, wide), lambda g, i: (0, g * steps + i)),
+            pl.BlockSpec((rows, HEAD_SIZE), lambda g, i: (0, g)),
+            pl.BlockSpec((rows, HEAD_SIZE), lambda g, i: (0, KEY_VALUE_HEADS + g)),
+            pl.BlockSpec((tokens, HEAD_SIZE), lambda g, i: (0, g)),
+            pl.BlockSpec((tokens, HEAD_SIZE), lambda g, i: (0, KEY_VALUE_HEADS + g)),
+        ],
+        out_specs=pl.BlockSpec((tokens, wide), lambda g, i: (0, g * steps + i)),
+        compiler_params=pltpu.CompilerParams(vmem_limit_bytes=40 * 1024 * 1024),
+    )(queries, prefix, prefix, local_kv, local_kv)
+
+
+def expert_kernel(row_ref, weight_ref, gate_ref, up_ref, down_ref, out_ref):
+    rows = row_ref[...]
+    gate = jnp.dot(rows, gate_ref[0], preferred_element_type=jnp.float32)
+    upper = jnp.dot(rows, up_ref[0], preferred_element_type=jnp.float32)
+    middle = (gate / (1.0 + jnp.exp(-gate)) * upper).astype(jnp.bfloat16)
+    answer = jnp.dot(middle, down_ref[0], preferred_element_type=jnp.float32)
+    answer = answer.astype(jnp.bfloat16).astype(jnp.float32)
+    out_ref[...] = (answer * weight_ref[...]).astype(out_ref.dtype)
+
+
+def run_expert(rows, weight, gate, up, down):
+    count, width = rows.shape
+    block = math.gcd(count, 256)
+    row_spec = pl.BlockSpec((block, width), lambda i: (i, 0))
+    return pl.pallas_call(
+        expert_kernel,
+        grid=(count // block,),
+        out_shape=jax.ShapeDtypeStruct(rows.shape, rows.dtype),
+        in_specs=[
+            row_spec,
+            pl.BlockSpec((block, 1), lambda i: (i, 0)),
+            pl.BlockSpec(gate.shape, lambda i: (0, 0, 0)),
+            pl.BlockSpec(up.shape, lambda i: (0, 0, 0)),
+            pl.BlockSpec(down.shape, lambda i: (0, 0, 0)),
+        ],
+        out_specs=row_spec,
+        compiler_params=pltpu.CompilerParams(vmem_limit_bytes=48 * 1024 * 1024),
+    )(rows, weight, gate, up, down)
+
+
 def attention(queries, local_kv, prefix):
     tokens = queries.shape[0]
     group = QUERY_HEADS // KEY_VALUE_HEADS
@@ -376,14 +497,20 @@
     if small:
         per_slot = jnp.pad(per_slot, ((0, 0), (0, -per_slot.shape[1] % 128)))
         prefix, projection, all_slots = gather(
-            levels, 0, document_prefix_cache, out_proj, per_slot
+            levels,
+            0,
+            document_prefix_cache,
+            out_proj,
+            per_slot,
+            shared=1 if lax.axis_size("group") == 2 else None,
         )
     else:
         prefix = lax.all_gather(document_prefix_cache, "line", axis=0, tiled=True)
         projection = lax.all_gather(out_proj, "line", axis=0, tiled=True)
         all_slots = lax.all_gather(per_slot, "line", axis=0, tiled=True)
     weight = lax.dynamic_slice_in_dim(all_slots, lax.axis_index("line"), 1, 1)
-    context = attention(queries, question_key_values, prefix)
+    mix = attend if small else attention
+    context = mix(queries, question_key_values, prefix)
     attended = jnp.dot(context, projection, preferred_element_type=jnp.float32)
     mixture = residual_in.astype(jnp.float32) + attended
     normed = (
@@ -393,11 +520,7 @@
         (rows,) = gather(levels, 1, normed)
     else:
         rows = lax.all_gather(normed, "line", axis=0, tiled=True)
-    gate = jnp.dot(rows, expert_gate[0], preferred_element_type=jnp.float32)
-    upper = jnp.dot(rows, expert_up[0], preferred_element_type=jnp.float32)
-    middle = (jax.nn.silu(gate) * upper).astype(jnp.bfloat16)
-    answer = jnp.dot(middle, expert_down[0], preferred_element_type=jnp.float32)
-    share = (answer.astype(jnp.bfloat16).astype(jnp.float32) * weight).astype(jnp.bfloat16)
+    share = run_expert(rows, weight, expert_gate, expert_up, expert_down)
     if small:
         summed = scatter(levels, 2, share)
     else:

time: 198 us -> 187 us (0.944)
  Pallas kernels: 138 us -> 169 us
  matrix products: 33.5 us -> 5.08 us
  local copies, waits for them, and re-layouts: 19 us -> 8.35 us
  other arithmetic: 6.73 us -> 3.87 us
    pallas_call x2 -> x4, Pallas kernels: 95 us -> 125 us  [the longest x2 105 us: gather(): pl.pallas_call(functools.partial(gather_kernel, levels, count, shared), o...]
    dot_general x6 -> x0, matrix products: 28.4 us -> none  [the longest x1 12.3 us: body(): answer = jnp.dot(middle, expert_down[0], preferred_element_type=jnp.float32)]
    slice x2 -> x0, local copies, waits for them, and re-layouts: 3.75 us -> none  [the longest x1 2.97 us: step(): keys = piece[:, :width].reshape(block, KEY_VALUE_HEADS, HEAD_SIZE)]
    unnamed x18, local copies, waits for them, and re-layouts: 9.81 us -> 6.41 us
    reduce_sum x2 -> x0, other arithmetic: 2.63 us -> none  [the longest x1 1.82 us: step(): return ((new_max, old_sum * factor + far.sum(-1), new_acc), None)]
where the time goes in v3:
time: 187 us; the launch traced here: 186 us
  Pallas kernels  169 us (90%)
  local copies, waits for them, and re-layouts  8.35 us (4%)
  matrix products  5.08 us (3%)
  other arithmetic  3.87 us (2%)
    pallas_call x2, Pallas kernels, gather(): pl.pallas_call(functools.partial(gather_kernel, levels, count, shared), o...  105 us
    pallas_call x1, Pallas kernels, scatter(): pl.pallas_call(functools.partial(scatter_kernel, levels), out_shape=jax.S...  43.5 us
    pallas_call x1, Pallas kernels, run_expert(): pl.pallas_call(expert_kernel, grid=(count // block,), out_shape=jax.Shape...  14.8 us
    unnamed x18, local copies, waits for them, and re-layouts  6.41 us
    pallas_call x1, Pallas kernels, attend(): pl.pallas_call(attend_kernel, grid=(KEY_VALUE_HEADS, steps), out_shape=ja...  5.76 us
    dot_general x1, matrix products, body(): attended = jnp.dot(context, projection, preferred_element_type=jnp.float32)  5.08 us

profile of v3, /device:TPU:10, one launch (start us, length us, event | category | flops | bytes accessed | tf_op | source)
XLA Modules:
  0.0 186.3 jit_solution(13801722172885635594)
XLA Ops:
  0.0 0.0 copy-start.7
  0.0 0.7 compare_select_fusion
  0.8 0.8 select_reduce_fusion.1
  1.5 0.8 select_reduce_fusion
  2.3 0.1 copy.16
  2.4 0.6 pad.4.refs_2_
  3.0 60.6 %shard_map.127 = (bf16[16,128,512]{2,1,0:T(8,128)(2,1)}, bf16[16,128,2048]{2,1,0:T(8,128)(2,1)}, f32[16,64,128]{2,1,0:T(8,128)}) custom-call(bf16[128,512]{1,0:T(8,128)(2,1)} %refs_0_.1, bf16[128,2048]{1,0:T(8,128)(2,1)} %refs_1_.1, f32[64,128]{1,0:T(8,128)} %pad.4.refs_2_), custom_call_target="tpu_custom_call" | custom-call | tf_op jit(solution)/shard_map/pallas_call | solution.py:183
  63.6 0.0 copy-start.1
  63.6 1.6 copy-done.1
  65.2 0.0 copy-start.3
  65.2 0.8 copy-done.3
  66.1 0.0 copy-start.4
  66.1 0.9 copy-done.4
  67.0 5.8 %shard_map.128 = bf16[64,2048]{1,0:T(8,128)(2,1)S(1)} custom-call(bf16[64,2048]{1,0:T(8,128)(2,1)S(1)} %copy-done.4, bf16[2048,512]{1,0:T(8,128)(2,1)S(1)} %bitcast.8, bf16[2048,512]{1,0:T(8,128)(2,1)S(1)} %bitcast.9, bf16[64,512]{1,0:T(8,128)(2,1)S(1)} %copy-done.3, bf16[64,512]{1,0:T(8,128)(2,1)S(1)} %copy-done.3), custom_call_target="tpu_custom_call" | custom-call | tf_op jit(solution)/shard_map/pallas_call | solution.py:381
  72.8 0.0 copy-done.7
  72.8 0.0 copy-start.8
  72.8 5.1 %multiply_reduce_fusion = (f32[64]{0:T(128)S(1)}, f32[64,2048]{1,0:T(8,128)S(1)}) fusion(bf16[64,2048]{1,0:T(8,128)(2,1)S(1)} %shard_map.128, bf16[2048,2048]{1,0:T(8,128)(2,1)} %bitcast.10, bf16[64,2048]{1,0:T(8,128)(2,1)S(1)} %copy-done.7), kind=kOutput, calls=%fused_computation.3 | convolution fusion | flops 537395136 | bytes 9437440 | tf_op jit(solution)/shard_map/dot_general | solution.py:514
  77.9 0.0 copy-start.5
  77.9 0.0 copy-start.2
  77.9 0.8 copy-done.5
  78.8 0.0 copy-done.8
  78.8 0.8 multiply_convert_fusion.refs_0_
  79.6 44.2 %shard_map.129 = bf16[16,64,2048]{2,1,0:T(8,128)(2,1)} custom-call(bf16[64,2048]{1,0:T(8,128)(2,1)} %multiply_convert_fusion.refs_0_), custom_call_target="tpu_custom_call" | custom-call | tf_op jit(solution)/shard_map/pallas_call | solution.py:183
  123.8 1.2 constant_dynamic-slice_fusion.weight_ref
  125.1 0.0 copy-done.2
  125.1 14.8 %shard_map.130 = bf16[1024,2048]{1,0:T(8,128)(2,1)} custom-call(bf16[1024,2048]{1,0:T(8,128)(2,1)} %bitcast.11, f32[1024,1]{1,0:T(8,128)S(1)} %constant_dynamic-slice_fusion.weight_ref, bf16[1,2048,768]{2,1,0:T(8,128)(2,1)S(1)} %copy-done.2, bf16[1,2048,768]{2,1,0:T(8,128)(2,1)} %up_ref.1, bf16[1,768,2048]{2,1,0:T(8,128)(2,1)} %down_ref.1), custom_call_target="tpu_custom_call" | custom-call | tf_op jit(solution)/shard_map/pallas_call | solution.py:411
  139.8 0.0 copy-start
  139.8 2.2 %copy-done = bf16[1024,2048]{1,0:T(8,128)(2,1)S(1)} copy-done((bf16[1024,2048]{1,0:T(8,128)(2,1)S(1)}, bf16[1024,2048]{1,0:T(8,128)(2,1)}, u32[]{:S(2)}) %copy-start) | copy-done | bytes 4194328
  142.0 0.0 copy-start.6
  142.0 43.5 %shard_map.131 = f32[64,2048]{1,0:T(8,128)S(1)} custom-call(bf16[16,64,2048]{2,1,0:T(8,128)(2,1)S(1)} %bitcast.7), custom_call_target="tpu_custom_call" | custom-call | tf_op jit(solution)/shard_map/pallas_call | solution.py:325
  185.6 0.0 copy-done.6
  185.6 0.8 add_convert_fusion
  (1 shorter events, 0.0 us)
Async XLA Ops:
  0.0 72.8 %copy-start.7 = (bf16[64,2048]{1,0:T(8,128)(2,1)S(1)}, bf16[64,2048]{1,0:T(8,128)(2,1)}, u32[]{:S(2)}) copy-start(bf16[64,2048]{1,0:T(8,128)(2,1)} %param.13) | copy-start | bytes 786436
  63.6 1.6 copy-start.1
  65.2 0.8 copy-start.3
  66.1 0.9 copy-start.4
  72.8 6.0 %copy-start.8 = (f32[2048]{0:T(1024)S(1)}, f32[2048]{0:T(1024)}, u32[]{:S(2)}) copy-start(f32[2048]{0:T(1024)} %param.18) | copy-start | bytes 24580
  77.9 0.9 copy-start.5
  77.9 47.2 %copy-start.2 = (bf16[1,2048,768]{2,1,0:T(8,128)(2,1)S(1)}, bf16[1,2048,768]{2,1,0:T(8,128)(2,1)}, u32[]{:S(2)}) copy-start(bf16[1,2048,768]{2,1,0:T(8,128)(2,1)} %gate_ref.1) | copy-start | bytes 9437188
  139.8 2.2 %copy-start = (bf16[1024,2048]{1,0:T(8,128)(2,1)S(1)}, bf16[1024,2048]{1,0:T(8,128)(2,1)}, u32[]{:S(2)}) copy-start(bf16[1024,2048]{1,0:T(8,128)(2,1)} %shard_map.130) | copy-start | bytes 12582916
  142.0 43.6 %copy-start.6 = (f32[64,2048]{1,0:T(8,128)S(1)}, f32[64,2048]{1,0:T(8,128)}, u32[]{:S(2)}) copy-start(f32[64,2048]{1,0:T(8,128)} %copy-done.5) | copy-start | bytes 1572868

commit v4 on v3

--- a/solution.py
+++ b/solution.py
@@ -502,7 +502,6 @@
             document_prefix_cache,
             out_proj,
             per_slot,
-            shared=1 if lax.axis_size("group") == 2 else None,
         )
     else:
         prefix = lax.all_gather(document_prefix_cache, "line", axis=0, tiled=True)

time: 187 us -> 177 us (0.947)
  Pallas kernels: 169 us -> 160 us
    pallas_call x2, Pallas kernels: 105 us -> 95.6 us  [gather(): pl.pallas_call(functools.partial(gather_kernel, levels, count, shared), o...]
where the time goes in v4:
time: 177 us
  Pallas kernels  160 us (90%)
  local copies, waits for them, and re-layouts  8.35 us (5%)
  matrix products  5.08 us (3%)
  other arithmetic  3.87 us (2%)
    pallas_call x2, Pallas kernels, gather(): pl.pallas_call(functools.partial(gather_kernel, levels, count, shared), o...  95.6 us
    pallas_call x1, Pallas kernels, scatter(): pl.pallas_call(functools.partial(scatter_kernel, levels), out_shape=jax.S...  43.5 us
    pallas_call x1, Pallas kernels, run_expert(): pl.pallas_call(expert_kernel, grid=(count // block,), out_shape=jax.Shape...  14.8 us
    unnamed x18, local copies, waits for them, and re-layouts  6.41 us
    pallas_call x1, Pallas kernels, attend(): pl.pallas_call(attend_kernel, grid=(KEY_VALUE_HEADS, steps), out_shape=ja...  5.75 us
    dot_general x1, matrix products, body(): attended = jnp.dot(context, projection, preferred_element_type=jnp.float32)  5.08 us

profile of v4, /device:TPU:10, one launch (start us, length us, event | category | flops | bytes accessed | tf_op | source)
XLA Modules:
  0.0 177.0 jit_solution(8465350471021010457)
XLA Ops:
  0.0 0.0 copy-start.7
  0.0 0.7 compare_select_fusion
  0.8 0.8 select_reduce_fusion.1
  1.5 0.8 select_reduce_fusion
  2.3 0.1 copy.16
  2.4 0.6 pad.4.refs_2_
  3.0 65.1 %shard_map.127 = (bf16[16,128,512]{2,1,0:T(8,128)(2,1)}, bf16[16,128,2048]{2,1,0:T(8,128)(2,1)}, f32[16,64,128]{2,1,0:T(8,128)}) custom-call(bf16[128,512]{1,0:T(8,128)(2,1)} %refs_0_.1, bf16[128,2048]{1,0:T(8,128)(2,1)} %refs_1_.1, f32[64,128]{1,0:T(8,128)} %pad.4.refs_2_), custom_call_target="tpu_custom_call" | custom-call | tf_op jit(solution)/shard_map/pallas_call | solution.py:183
  68.1 0.0 copy-start.1
  68.1 1.6 copy-done.1
  69.7 0.0 copy-start.3
  69.7 0.8 copy-done.3
  70.5 0.0 copy-start.4
  70.5 0.9 copy-done.4
  71.5 5.8 %shard_map.128 = bf16[64,2048]{1,0:T(8,128)(2,1)S(1)} custom-call(bf16[64,2048]{1,0:T(8,128)(2,1)S(1)} %copy-done.4, bf16[2048,512]{1,0:T(8,128)(2,1)S(1)} %bitcast.8, bf16[2048,512]{1,0:T(8,128)(2,1)S(1)} %bitcast.9, bf16[64,512]{1,0:T(8,128)(2,1)S(1)} %copy-done.3, bf16[64,512]{1,0:T(8,128)(2,1)S(1)} %copy-done.3), custom_call_target="tpu_custom_call" | custom-call | tf_op jit(solution)/shard_map/pallas_call | solution.py:381
  77.2 0.0 copy-done.7
  77.2 0.0 copy-start.8
  77.2 5.1 %multiply_reduce_fusion = (f32[64]{0:T(128)S(1)}, f32[64,2048]{1,0:T(8,128)S(1)}) fusion(bf16[64,2048]{1,0:T(8,128)(2,1)S(1)} %shard_map.128, bf16[2048,2048]{1,0:T(8,128)(2,1)} %bitcast.10, bf16[64,2048]{1,0:T(8,128)(2,1)S(1)} %copy-done.7), kind=kOutput, calls=%fused_computation.3 | convolution fusion | flops 537395136 | bytes 9437440 | tf_op jit(solution)/shard_map/dot_general | solution.py:513
  82.3 0.0 copy-start.5
  82.3 0.0 copy-start.2
  82.4 0.8 copy-done.5
  83.2 0.0 copy-done.8
  83.2 0.8 multiply_convert_fusion.refs_0_
  84.0 30.5 %shard_map.129 = bf16[16,64,2048]{2,1,0:T(8,128)(2,1)} custom-call(bf16[64,2048]{1,0:T(8,128)(2,1)} %multiply_convert_fusion.refs_0_), custom_call_target="tpu_custom_call" | custom-call | tf_op jit(solution)/shard_map/pallas_call | solution.py:183
  114.5 1.2 constant_dynamic-slice_fusion.weight_ref
  115.8 0.0 copy-done.2
  115.8 14.8 %shard_map.130 = bf16[1024,2048]{1,0:T(8,128)(2,1)} custom-call(bf16[1024,2048]{1,0:T(8,128)(2,1)} %bitcast.11, f32[1024,1]{1,0:T(8,128)S(1)} %constant_dynamic-slice_fusion.weight_ref, bf16[1,2048,768]{2,1,0:T(8,128)(2,1)S(1)} %copy-done.2, bf16[1,2048,768]{2,1,0:T(8,128)(2,1)} %up_ref.1, bf16[1,768,2048]{2,1,0:T(8,128)(2,1)} %down_ref.1), custom_call_target="tpu_custom_call" | custom-call | tf_op jit(solution)/shard_map/pallas_call | solution.py:411
  130.5 0.0 copy-start
  130.5 2.2 %copy-done = bf16[1024,2048]{1,0:T(8,128)(2,1)S(1)} copy-done((bf16[1024,2048]{1,0:T(8,128)(2,1)S(1)}, bf16[1024,2048]{1,0:T(8,128)(2,1)}, u32[]{:S(2)}) %copy-start) | copy-done | bytes 4194328
  132.7 0.0 copy-start.6
  132.7 43.5 %shard_map.131 = f32[64,2048]{1,0:T(8,128)S(1)} custom-call(bf16[16,64,2048]{2,1,0:T(8,128)(2,1)S(1)} %bitcast.7), custom_call_target="tpu_custom_call" | custom-call | tf_op jit(solution)/shard_map/pallas_call | solution.py:325
  176.2 0.0 copy-done.6
  176.2 0.8 add_convert_fusion
  (1 shorter events, 0.0 us)
Async XLA Ops:
  0.0 77.2 %copy-start.7 = (bf16[64,2048]{1,0:T(8,128)(2,1)S(1)}, bf16[64,2048]{1,0:T(8,128)(2,1)}, u32[]{:S(2)}) copy-start(bf16[64,2048]{1,0:T(8,128)(2,1)} %param.13) | copy-start | bytes 786436
  68.1 1.6 copy-start.1
  69.7 0.8 copy-start.3
  70.5 0.9 copy-start.4
  77.2 6.0 %copy-start.8 = (f32[2048]{0:T(1024)S(1)}, f32[2048]{0:T(1024)}, u32[]{:S(2)}) copy-start(f32[2048]{0:T(1024)} %param.18) | copy-start | bytes 24580
  82.3 0.9 copy-start.5
  82.3 33.4 %copy-start.2 = (bf16[1,2048,768]{2,1,0:T(8,128)(2,1)S(1)}, bf16[1,2048,768]{2,1,0:T(8,128)(2,1)}, u32[]{:S(2)}) copy-start(bf16[1,2048,768]{2,1,0:T(8,128)(2,1)} %gate_ref.1) | copy-start | bytes 9437188
  130.5 2.2 %copy-start = (bf16[1024,2048]{1,0:T(8,128)(2,1)S(1)}, bf16[1024,2048]{1,0:T(8,128)(2,1)}, u32[]{:S(2)}) copy-start(bf16[1024,2048]{1,0:T(8,128)(2,1)} %shard_map.130) | copy-start | bytes 12582916
  132.7 43.5 %copy-start.6 = (f32[64,2048]{1,0:T(8,128)S(1)}, f32[64,2048]{1,0:T(8,128)}, u32[]{:S(2)}) copy-start(f32[64,2048]{1,0:T(8,128)} %copy-done.5) | copy-start | bytes 1572868
